TPU v7x, 128 devices: a whole 4x4x4 slice. The times are simulated.
128 devices in a mesh: gallery: 32 (over x, y, core), query: 4 (over z).
Axes of the slice: x: 4, y: 4, z: 4, core: 2. Of those that a mesh axis runs over, the one named last changes fastest.
Arguments:
- text_states: bfloat16 [4096, 32, 768], P(('gallery', 'query')), may hold values from -50 to 50
- caption_aligned_vector: bfloat16 [4096, 256], P(('gallery', 'query')), may hold values from -0.375 to 0.375
- cluster_list: int32 [4096, 8], P(('gallery', 'query')), may hold values from 0 to 255
- pair_image: int32 [4096, 16], P(('gallery', 'query')), may hold values from 0 to 511, as said below
- image_keys: bfloat16 [512, 577, 768], P(('gallery', 'query')), may hold values from -368 to 368
- image_values: bfloat16 [512, 577, 768], P(('gallery', 'query')), may hold values from -6 to 6
- picture_aligned_vector: bfloat16 [512, 256], P(('gallery', 'query')), may hold values from -6 to 6
- w_self_q: bfloat16 [768, 768], replicated, may hold values from -0.21875 to 0.21875
- w_self_k: bfloat16 [768, 768], replicated, may hold values from -0.21875 to 0.21875
- w_self_v: bfloat16 [768, 768], replicated, may hold values from -0.21875 to 0.21875
- w_self_o: bfloat16 [768, 768], replicated, may hold values from -0.21875 to 0.21875
- w_cross_q: bfloat16 [768, 768], replicated, may hold values from -0.21875 to 0.21875
- w_cross_o: bfloat16 [768, 768], replicated, may hold values from -0.21875 to 0.21875
- w_up: bfloat16 [768, 3072], replicated, may hold values from -0.21875 to 0.21875
- w_down: bfloat16 [3072, 768], replicated, may hold values from -0.109375 to 0.109375
- itm_head: bfloat16 [768, 2], replicated, may hold values from -0.21875 to 0.21875
Outputs:
- rerank: float32 [4096, 16], P(('gallery', 'query'))
Inputs may be any that keep to these rules, and one draw needn't show every extreme that they name: `pair_image`: images j * 4 to (j + 1) * 4 - 1 form shard j. Among the 512 pairs of the queries n * 32 to (n + 1) * 32 - 1, at most 5 have their image in any one shard, and in every draw one shard holds exactly 5 of them for every n. A query may name an image twice.
All inputs are finite; a program needn't handle non-finite values.
Results may differ from a plain program's by a relative error of at most 0.0024.
Values may be sent and summed in bfloat16 or wider, within the bound.
A program may use at most 256 MiB of HBM per device.

v0:
```python
import jax
import jax.numpy as jnp
from jax import lax
from jax.sharding import PartitionSpec as P

HEADS = 12
BLOCK_IMG = 2


norm_epsilon = 1e-06
inverse_softness_factor = 1.0 / 0.07


def combined_all(value, axis, join):
    pieces = jax.tree.map(lambda part: lax.all_gather(part, axis), value)
    head = jax.tree.map(lambda part: part[0], pieces)
    tail = jax.tree.map(lambda part: part[1:], pieces)
    total, _ = lax.scan(lambda total, share: (join(total, share), None), head, tail)
    return total


def layer_norm(inputs):
    centered = inputs - jnp.mean(inputs, axis=-1, keepdims=True)
    variance = jnp.mean(centered * centered, axis=-1, keepdims=True)
    return centered * lax.rsqrt(variance + norm_epsilon)


def itm_logits(state, w_up, w_down, itm_head):
    hidden = jax.nn.gelu(
        jnp.dot(state, w_up, preferred_element_type=jnp.float32), approximate=False
    ).astype(jnp.bfloat16)
    mixed_state = layer_norm(
        state.astype(jnp.float32) + jnp.dot(hidden, w_down, preferred_element_type=jnp.float32)
    ).astype(jnp.bfloat16)
    return jnp.dot(mixed_state, itm_head, preferred_element_type=jnp.float32)


def summary_focus_weights(text_states, w_self_q, w_self_k, w_self_v, w_self_o):
    query_total, text_length, features = text_states.shape
    head_size = features // HEADS
    first_token = text_states[:, 0, :]
    cls_query = jnp.dot(first_token, w_self_q, preferred_element_type=jnp.float32).astype(
        jnp.bfloat16
    )
    flat_rows = text_states.reshape(query_total * text_length, features)
    key_rows = jnp.dot(flat_rows, w_self_k, preferred_element_type=jnp.float32).astype(jnp.bfloat16)
    value_rows = jnp.dot(flat_rows, w_self_v, preferred_element_type=jnp.float32).astype(
        jnp.bfloat16
    )
    cls_query = cls_query.reshape(query_total, HEADS, head_size)
    key_rows = key_rows.reshape(query_total, text_length, HEADS, head_size)
    value_rows = value_rows.reshape(query_total, text_length, HEADS, head_size)
    scores = jnp.einsum(
        "nhd,nthd->nht", cls_query, key_rows, preferred_element_type=jnp.float32
    ) * head_size ** (-0.5)
    weights = jax.nn.softmax(scores, axis=-1).astype(jnp.bfloat16)
    context = jnp.einsum("nht,nthd->nhd", weights, value_rows, preferred_element_type=jnp.float32)
    context = context.astype(jnp.bfloat16).reshape(query_total, features)
    attended = jnp.dot(context, w_self_o, preferred_element_type=jnp.float32)
    return layer_norm(first_token.astype(jnp.float32) + attended).astype(jnp.bfloat16)


def combine_totals(former, latter):
    top_value = jnp.maximum(former[0], latter[0])
    return (
        top_value,
        former[1] * jnp.exp(former[0] - top_value) + latter[1] * jnp.exp(latter[0] - top_value),
    )


def slot_table(owner_index, devices, capacity):
    pair_total = owner_index.shape[0]
    device_range = jnp.arange(devices, dtype=jnp.int32)
    owner_marks = (owner_index[:, None] == device_range[None, :]).astype(jnp.int32)
    slot_rank = jnp.sum((jnp.cumsum(owner_marks, axis=0) - 1) * owner_marks, axis=1)
    slot_match = (owner_index[None, None, :] == device_range[:, None, None]) & (
        slot_rank[None, None, :] == jnp.arange(capacity, dtype=jnp.int32)[None, :, None]
    )
    slot_pair = jnp.sum(
        jnp.where(slot_match, jnp.arange(pair_total, dtype=jnp.int32)[None, None, :], 0), axis=2
    )
    return (slot_rank, slot_pair)


def local(
    text_states,
    caption_aligned_vector,
    cluster_list,
    pair_image,
    image_keys,
    image_values,
    picture_aligned_vector,
    w_self_q,
    w_self_k,
    w_self_v,
    w_self_o,
    w_cross_q,
    w_cross_o,
    w_up,
    w_down,
    itm_head,
):
    groups = lax.axis_size("gallery")
    members = lax.axis_size("query")
    devices = groups * members
    position = lax.axis_index(("gallery", "query"))
    query_count, text_length, features = text_states.shape
    per_query = pair_image.shape[1]
    local_images = image_keys.shape[0]
    image_tokens = image_keys.shape[1]
    pair_total = query_count * per_query
    capacity = 5 * pair_total // (4 * devices)
    head_size = features // HEADS
    leading_token_state = summary_focus_weights(text_states, w_self_q, w_self_k, w_self_v, w_self_o)
    all_itc, all_lists = (
        lax.all_gather(caption_aligned_vector, ("gallery", "query"), axis=0, tiled=True),
        lax.all_gather(cluster_list, ("gallery", "query"), axis=0, tiled=True),
    )
    local_scores = (
        lax.dot_general(
            all_itc,
            picture_aligned_vector,
            (((1,), (1,)), ((), ())),
            preferred_element_type=jnp.float32,
        )
        * inverse_softness_factor
    )
    image_index = position * local_images + jnp.arange(local_images, dtype=jnp.int32)
    listed = jnp.any(all_lists[:, :, None] == (image_index // BLOCK_IMG)[None, None, :], axis=1)
    masked = jnp.where(listed, local_scores, -1e30)
    part_top = jnp.max(masked, axis=1)
    part_sum = jnp.sum(jnp.where(listed, jnp.exp(masked - part_top[:, None]), 0.0), axis=1)
    whole_top, whole_sum = combined_all((part_top, part_sum), ("gallery", "query"), combine_totals)
    own_top = lax.dynamic_slice_in_dim(whole_top, position * query_count, query_count)
    own_sum = lax.dynamic_slice_in_dim(whole_sum, position * query_count, query_count)
    itc_total = own_top + jnp.log(own_sum)
    owner_index = (pair_image // local_images).reshape(pair_total)
    local_pick = (pair_image % local_images).reshape(pair_total)
    slot_rank, slot_pair = slot_table(owner_index, devices, capacity)
    slot_query = slot_pair // per_query
    send_rows = leading_token_state[slot_query]
    send_info = jnp.stack([position * query_count + slot_query, local_pick[slot_pair]], axis=-1)
    rows_in = lax.all_to_all(
        send_rows, ("gallery", "query"), split_axis=0, concat_axis=0, tiled=True
    )
    info_in = lax.all_to_all(
        send_info, ("gallery", "query"), split_axis=0, concat_axis=0, tiled=True
    )
    sources = rows_in.shape[0]
    slot_total = rows_in.shape[1]
    flat_rows = rows_in.reshape(sources * slot_total, features)
    image_ids = info_in[:, :, 1].reshape(-1)
    cross_query = jnp.dot(flat_rows, w_cross_q, preferred_element_type=jnp.float32).astype(
        jnp.bfloat16
    )
    cross_query = cross_query.reshape(-1, HEADS, head_size)
    context = jnp.zeros((flat_rows.shape[0], HEADS, head_size), jnp.float32)
    for number in range(local_images):
        key_rows = image_keys[number].reshape(image_tokens, HEADS, head_size)
        value_rows = image_values[number].reshape(image_tokens, HEADS, head_size)
        scores = jnp.einsum(
            "rhd,thd->rht", cross_query, key_rows, preferred_element_type=jnp.float32
        ) * head_size ** (-0.5)
        weights = jax.nn.softmax(scores, axis=-1).astype(jnp.bfloat16)
        attended = jnp.einsum(
            "rht,thd->rhd", weights, value_rows, preferred_element_type=jnp.float32
        )
        context = jnp.where((image_ids == number)[:, None, None], attended, context)
    context = context.astype(jnp.bfloat16).reshape(-1, features)
    cross_state = layer_norm(
        flat_rows.astype(jnp.float32)
        + jnp.dot(context, w_cross_o, preferred_element_type=jnp.float32)
    ).astype(jnp.bfloat16)
    back_state, back_image = (
        lax.all_to_all(
            cross_state.reshape(sources, slot_total, features),
            ("gallery", "query"),
            split_axis=0,
            concat_axis=0,
            tiled=True,
        ),
        lax.all_to_all(
            picture_aligned_vector[image_ids].reshape(sources, slot_total, -1),
            ("gallery", "query"),
            split_axis=0,
            concat_axis=0,
            tiled=True,
        ),
    )
    logits = itm_logits(back_state[owner_index, slot_rank], w_up, w_down, itm_head)
    text_rows = jnp.repeat(caption_aligned_vector, per_query, axis=0)
    pair_itc = (
        jnp.einsum(
            "pe,pe->p",
            text_rows,
            back_image[owner_index, slot_rank],
            preferred_element_type=jnp.float32,
        )
        * inverse_softness_factor
    )
    margin = logits[:, 1] - logits[:, 0] + pair_itc
    return margin.reshape(query_count, per_query) - itc_total[:, None]


def solution(mesh):
    return jax.shard_map(
        local,
        mesh=mesh,
        in_specs=(
            P(("gallery", "query"), None, None),
            P(("gallery", "query"), None),
            P(("gallery", "query"), None),
            P(("gallery", "query"), None),
            P(("gallery", "query"), None, None),
            P(("gallery", "query"), None, None),
            P(("gallery", "query"), None),
            P(),
            P(),
            P(),
            P(),
            P(),
            P(),
            P(),
            P(),
            P(),
        ),
        out_specs=P(("gallery", "query"), None),
        check_vma=False,
    )
```

profile of v0, /device:TPU:1, one launch (start us, length us, event | category | flops | bytes accessed | tf_op | source)
XLA Modules:
  0.0 560.0 jit_solution(3394201887441646312)
XLA Ops:
  16.2 11.8 %all-to-all-start.1 = ((s32[128,5,2]{1,2,0:T(2,128)}), s32[128,5,2]{1,2,0:T(2,128)S(1)}, u32[]{:S(2)}, u32[]{:S(2)}) async-start(s32[128,5,2]{1,2,0:T(2,128)} %copy.87), calls=%async_computation.1 | async-start | bytes 262144 | tf_op jit(solution)/shard_map/all_to_all | solution.py:146
  37.0 5.9 %reshape.354 = bf16[32,32,12,64]{3,2,1,0:T(8,128)(2,1)} reshape(bf16[1024,768]{1,0:T(8,128)(2,1)} %convolution_convert_fusion) | data formatting | bytes 3145728 | tf_op jit(solution)/shard_map/reshape | solution.py:52
  54.9 11.6 %fusion.126 = (bf16[1,577,768]{2,0,1:T(2,128)(2,1)}, bf16[1,577,768]{2,0,1:T(2,128)(2,1)}, bf16[1,577,768]{2,0,1:T(2,128)(2,1)}, bf16[1,577,768]{2,0,1:T(2,128)(2,1)}) fusion(bf16[4,577,768]{2,0,1:T(4,128)(2,1)} %param.22), kind=kLoop, calls=%fused_computation.209 | loop fusion | bytes 7090176 | tf_op jit(solution)/shard_map/slice | solution.py:159
  66.6 6.3 %fusion.127 = (bf16[1,577,768]{2,0,1:T(2,128)(2,1)}, bf16[1,577,768]{2,0,1:T(2,128)(2,1)}, bf16[1,577,768]{2,0,1:T(2,128)(2,1)}, bf16[1,577,768]{2,0,1:T(2,128)(2,1)S(1)}) fusion(bf16[4,577,768]{2,0,1:T(4,128)(2,1)S(1)} %copy-done.3), kind=kLoop, calls=%fused_computation.210 | loop fusion | bytes 7090176 | tf_op jit(solution)/shard_map/slice | solution.py:160
  77.4 10.3 %all-to-all-start = ((bf16[128,5,768]{2,1,0:T(8,128)(2,1)}), bf16[128,5,768]{2,1,0:T(8,128)(2,1)}, u32[]{:S(2)}, u32[]{:S(2)}) async-start(bf16[128,5,768]{2,1,0:T(8,128)(2,1)} %reshape.367), calls=%async_computation | async-start | bytes 3145728 | tf_op jit(solution)/shard_map/all_to_all | solution.py:143
  87.6 64.1 %all-gather.2 = s32[128,32,8]{1,2,0:T(8,128)S(1)} all-gather(s32[1,32,8]{1,2,0:T(8,128)S(1)} %bitcast.190), channel_id=1, replica_groups=mesh['gallery'=32,'query'=4] {'gallery','query'}, dimensions={0}, use_global_device_ids=true | all-gather | bytes 132096 | tf_op jit(solution)/shard_map/all_gather | solution.py:117
  166.6 4.8 copy.97
  171.4 4.8 copy.101
  176.3 4.8 copy.95
  181.1 4.8 copy.92
  195.5 6.5 %all-to-all-start.3 = ((bf16[128,5,256]{2,1,0:T(8,128)(2,1)}), bf16[128,5,256]{2,1,0:T(8,128)(2,1)S(1)}, u32[]{:S(2)}, u32[]{:S(2)}) async-start(bf16[128,5,256]{2,1,0:T(8,128)(2,1)} %reshape.363), calls=%async_computation.3 | async-start | bytes 1048576 | tf_op jit(solution)/shard_map/all_to_all | solution.py:182
  210.2 10.1 %fusion.131 = (f32[640,12]{0,1:T(8,128)S(1)}, f32[640,12,577]{0,2,1:T(8,128)}) fusion(bf16[640,12,64]{0,2,1:T(8,128)(2,1)} %bitcast.181, bf16[577,12,64]{0,2,1:T(8,128)(2,1)S(1)} %bitcast.180), kind=kOutput, calls=%fused_computation.214 | convolution fusion | flops 580508736 | bytes 19625472 | tf_op jit(solution)/shard_map/sub | solution.py:164
  220.2 10.2 %fusion.129 = (f32[640,12]{0,1:T(8,128)S(1)}, f32[640,12,577]{0,2,1:T(8,128)}) fusion(bf16[640,12,64]{0,2,1:T(8,128)(2,1)} %bitcast.182, bf16[577,12,64]{0,2,1:T(8,128)(2,1)S(1)} %bitcast.178), kind=kOutput, calls=%fused_computation.212 | convolution fusion | flops 580508736 | bytes 19625472 | tf_op jit(solution)/shard_map/sub | solution.py:164
  230.4 10.1 %fusion.130 = (f32[640,12]{0,1:T(8,128)S(1)}, f32[640,12,577]{0,2,1:T(8,128)}) fusion(bf16[640,12,64]{0,2,1:T(8,128)(2,1)} %bitcast.183, bf16[577,12,64]{0,2,1:T(8,128)(2,1)S(1)} %bitcast.177), kind=kOutput, calls=%fused_computation.213 | convolution fusion | flops 580508736 | bytes 19625472 | tf_op jit(solution)/shard_map/sub | solution.py:164
  240.5 10.3 %fusion.132 = (f32[640,12]{0,1:T(8,128)S(1)}, f32[640,12,577]{0,2,1:T(8,128)}) fusion(bf16[640,12,64]{0,2,1:T(8,128)(2,1)} %bitcast.184, bf16[577,12,64]{0,2,1:T(8,128)(2,1)S(1)} %bitcast.175), kind=kOutput, calls=%fused_computation.215 | convolution fusion | flops 580508736 | bytes 19625472 | tf_op jit(solution)/shard_map/sub | solution.py:164
  250.8 8.8 %fusion.32 = bf16[12,640,64]{1,2,0:T(8,128)(2,1)} fusion(bf16[577,12,64]{0,2,1:T(8,128)(2,1)S(1)} %bitcast.179, f32[640,12,577]{0,2,1:T(8,128)} %get-tuple-element.75, f32[640,12]{0,1:T(8,128)S(1)} %get-tuple-element.74), kind=kOutput, calls=%fused_computation.45 | convolution fusion | flops 576076800 | bytes 19625472 | tf_op jit(solution)/shard_map/rht,thd->rhd/dot_general | solution.py:165
  259.6 8.9 %fusion.30 = bf16[12,640,64]{1,2,0:T(8,128)(2,1)} fusion(bf16[577,12,64]{0,2,1:T(8,128)(2,1)S(1)} %bitcast.176, f32[640,12,577]{0,2,1:T(8,128)} %get-tuple-element.71, f32[640,12]{0,1:T(8,128)S(1)} %get-tuple-element.70), kind=kOutput, calls=%fused_computation.43 | convolution fusion | flops 576076800 | bytes 19625472 | tf_op jit(solution)/shard_map/rht,thd->rhd/dot_general | solution.py:165
  268.5 8.9 %fusion.31 = bf16[12,640,64]{1,2,0:T(8,128)(2,1)} fusion(bf16[577,12,64]{0,2,1:T(8,128)(2,1)S(1)} %bitcast.174, f32[640,12,577]{0,2,1:T(8,128)} %get-tuple-element.73, f32[640,12]{0,1:T(8,128)S(1)} %get-tuple-element.72), kind=kOutput, calls=%fused_computation.44 | convolution fusion | flops 576076800 | bytes 19625472 | tf_op jit(solution)/shard_map/rht,thd->rhd/dot_general | solution.py:165
  280.3 8.2 %select_convert_fusion = bf16[12,640,64]{1,2,0:T(8,128)(2,1)S(1)} fusion(bf16[12,640,64]{1,2,0:T(8,128)(2,1)} %fusion.30, bf16[12,640,64]{1,2,0:T(8,128)(2,1)} %fusion.31, bf16[12,640,64]{1,2,0:T(8,128)(2,1)} %fusion.32, bf16[577,12,64]{0,2,1:T(8,128)(2,1)S(1)} %bitcast.173, f32[640,12,577]{0,2,1:T(8,128)} %get-tuple-element.77, ...), kind=kOutput, calls=%fused_computation.78 | convolution fusion | flops 578042880 | bytes 22577152 | tf_op jit(solution)/shard_map/rht,thd->rhd/dot_general | solution.py:165
  291.7 9.8 %all-to-all-start.2 = ((bf16[128,5,768]{2,1,0:T(8,128)(2,1)}), bf16[128,5,768]{2,1,0:T(8,128)(2,1)S(1)}, u32[]{:S(2)}, u32[]{:S(2)}) async-start(bf16[128,5,768]{2,1,0:T(8,128)(2,1)} %reshape.361), calls=%async_computation.2 | async-start | bytes 3145728 | tf_op jit(solution)/shard_map/all_to_all | solution.py:175
  304.9 22.0 %all-to-all-done.2 = bf16[128,5,768]{2,1,0:T(8,128)(2,1)S(1)} async-done(((bf16[128,5,768]{2,1,0:T(8,128)(2,1)}), bf16[128,5,768]{2,1,0:T(8,128)(2,1)S(1)}, u32[]{:S(2)}, u32[]{:S(2)}) %all-to-all-start.2) | async-done | bytes 983072 | tf_op jit(solution)/shard_map/all_to_all | solution.py:175
  332.6 21.0 %fusion.134 = (f32[512]{0:T(512)S(1)}, f32[512,768]{1,0:T(8,128)S(1)}) fusion(bf16[3072,768]{1,0:T(8,128)(2,1)} %param.32, bf16[512,768]{1,0:T(8,128)(2,1)S(1)} %gather_fusion.2, bf16[768,3072]{1,0:T(8,128)(2,1)} %param.31), kind=kOutput, calls=%fused_computation.217 | convolution fusion | flops 4935253504 | bytes 11798528 | tf_op jit(solution)/shard_map/dot_general | solution.py:33
  358.0 58.8 %all-gather.11.cloned.1.call-done = f32[524288]{0:T(1024)} async-done(((f32[4096]{0:T(1024)}), f32[524288]{0:T(1024)}) %all-gather.11.cloned.1.call-update) | async-done | bytes 2097168 | tf_op jit(solution)/shard_map/all_gather | solution.py:15
  420.2 132.2 %while.12 = (s32[]{:T(128)}, f32[4096]{0:T(1024)S(1)}, f32[4096]{0:T(1024)S(1)}, f32[127,4096]{1,0:T(8,128)}, f32[127,4096]{1,0:T(8,128)}, /*index=5*/s32[]{:T(128)}) while((s32[]{:T(128)}, f32[4096]{0:T(1024)S(1)}, f32[4096]{0:T(1024)S(1)}, f32[127,4096]{1,0:T(8,128)}, f32[127,4096]{1,0:T(8,128)}, /*index=5*/s32[]{:T(128)}) %tuple.55), condition=%wide.region_24.25_spmd, body=%wide.region_23.24_spmd.sunk | while | flops 24578 | bytes 163921 | solution.py:18
  (422 shorter events, 220.6 us)
Async XLA Ops:
  6.5 23.3 %copy-start = (bf16[768,768]{1,0:T(8,128)(2,1)S(1)}, bf16[768,768]{1,0:T(8,128)(2,1)}, u32[]{:S(2)}) copy-start(bf16[768,768]{1,0:T(8,128)(2,1)} %param.26) | copy-start | bytes 3538948
  6.5 270.9 %all-gather.7.cloned.1.call-start = ((), (), s32[]{:S(2)}) async-start(), calls=%async_computation.4 | async-start | bytes 2113536 | tf_op jit(solution)/shard_map/all_gather | solution.py:116
  10.8 18.3 %copy-start.4 = (bf16[768,768]{1,0:T(8,128)(2,1)S(1)}, bf16[768,768]{1,0:T(8,128)(2,1)}, u32[]{:S(2)}) copy-start(bf16[768,768]{1,0:T(8,128)(2,1)} %param.25) | copy-start | bytes 3538948
  16.2 61.1 %all-to-all-start.1 = ((s32[128,5,2]{1,2,0:T(2,128)}), s32[128,5,2]{1,2,0:T(2,128)S(1)}, u32[]{:S(2)}, u32[]{:S(2)}) async-start(s32[128,5,2]{1,2,0:T(2,128)} %copy.87), calls=%async_computation.1 | async-start | bytes 262144 | tf_op jit(solution)/shard_map/all_to_all | solution.py:146
  42.9 11.3 %copy-start.5 = (bf16[768,768]{1,0:T(8,128)(2,1)S(1)}, bf16[768,768]{1,0:T(8,128)(2,1)}, u32[]{:S(2)}) copy-start(bf16[768,768]{1,0:T(8,128)(2,1)} %param.28) | copy-start | bytes 3538948
  54.9 11.7 %copy-start.3 = (bf16[4,577,768]{2,0,1:T(4,128)(2,1)S(1)}, bf16[4,577,768]{2,0,1:T(4,128)(2,1)}, u32[]{:S(2)}) copy-start(bf16[4,577,768]{2,0,1:T(4,128)(2,1)} %param.23) | copy-start | bytes 10635268
  72.9 14.7 %copy-start.22 = (s32[32,8]{0,1:T(8,128)S(1)}, s32[32,8]{0,1:T(8,128)}, u32[]{:S(2)}) copy-start(s32[32,8]{0,1:T(8,128)} %param.20) | copy-start | bytes 3076
  77.4 118.2 %all-to-all-start = ((bf16[128,5,768]{2,1,0:T(8,128)(2,1)}), bf16[128,5,768]{2,1,0:T(8,128)(2,1)}, u32[]{:S(2)}, u32[]{:S(2)}) async-start(bf16[128,5,768]{2,1,0:T(8,128)(2,1)} %reshape.367), calls=%async_computation | async-start | bytes 3145728 | tf_op jit(solution)/shard_map/all_to_all | solution.py:143
  171.4 20.3 %copy-start.2 = (bf16[4,256]{1,0:T(4,128)(2,1)S(1)}, bf16[4,256]{1,0:T(4,128)(2,1)}, u32[]{:S(2)}) copy-start(bf16[4,256]{1,0:T(4,128)(2,1)} %param.24) | copy-start | bytes 6148
  195.5 14.7 %copy-start.13 = (bf16[1,577,768]{1,2,0:T(8,128)(2,1)S(1)}, bf16[1,577,768]{1,2,0:T(8,128)(2,1)}, u32[]{:S(2)}) copy-start(bf16[1,577,768]{1,2,0:T(8,128)(2,1)} %copy.97) | copy-start | bytes 2658820
  195.5 96.1 %all-to-all-start.3 = ((bf16[128,5,256]{2,1,0:T(8,128)(2,1)}), bf16[128,5,256]{2,1,0:T(8,128)(2,1)S(1)}, u32[]{:S(2)}, u32[]{:S(2)}) async-start(bf16[128,5,256]{2,1,0:T(8,128)(2,1)} %reshape.363), calls=%async_computation.3 | async-start | bytes 1048576 | tf_op jit(solution)/shard_map/all_to_all | solution.py:182
  202.0 152.4 %all-gather.9.cloned.1.call-start = ((), (), s32[]{:S(2)}) async-start(), calls=%async_computation.5 | async-start | bytes 2113536 | tf_op jit(solution)/shard_map/all_gather | solution.py:15
  220.2 10.2 %copy-start.10 = (bf16[1,577,768]{1,2,0:T(8,128)(2,1)S(1)}, bf16[1,577,768]{1,2,0:T(8,128)(2,1)}, u32[]{:S(2)}) copy-start(bf16[1,577,768]{1,2,0:T(8,128)(2,1)} %copy.94) | copy-start | bytes 2658820
  240.5 10.3 %copy-start.12 = (bf16[1,577,768]{1,2,0:T(8,128)(2,1)S(1)}, bf16[1,577,768]{1,2,0:T(8,128)(2,1)}, u32[]{:S(2)}) copy-start(bf16[1,577,768]{1,2,0:T(8,128)(2,1)} %copy.98) | copy-start | bytes 2658820
  268.5 11.8 %copy-start.6 = (bf16[1,577,768]{1,2,0:T(8,128)(2,1)S(1)}, bf16[1,577,768]{1,2,0:T(8,128)(2,1)}, u32[]{:S(2)}) copy-start(bf16[1,577,768]{1,2,0:T(8,128)(2,1)} %copy.101) | copy-start | bytes 2658820
  289.6 11.9 %copy-start.17 = (s32[32,16]{1,0:T(8,128)S(1)}, s32[32,16]{1,0:T(8,128)}, u32[]{:S(2)}) copy-start(s32[32,16]{1,0:T(8,128)} %copy-done.16) | copy-start | bytes 6148
  289.6 11.9 %copy-start.21 = (s32[512]{0:T(512)S(1)}, s32[512]{0:T(512)}, u32[]{:S(2)}) copy-start(s32[512]{0:T(512)} %copy-done.20) | copy-start | bytes 6148
  290.0 14.7 %copy-start.19 = (bf16[32,256]{1,0:T(8,128)(2,1)S(1)}, bf16[32,256]{1,0:T(8,128)(2,1)}, u32[]{:S(2)}) copy-start(bf16[32,256]{1,0:T(8,128)(2,1)} %param.19) | copy-start | bytes 49156
  291.7 35.3 %all-to-all-start.2 = ((bf16[128,5,768]{2,1,0:T(8,128)(2,1)}), bf16[128,5,768]{2,1,0:T(8,128)(2,1)S(1)}, u32[]{:S(2)}, u32[]{:S(2)}) async-start(bf16[128,5,768]{2,1,0:T(8,128)(2,1)} %reshape.361), calls=%async_computation.2 | async-start | bytes 3145728 | tf_op jit(solution)/shard_map/all_to_all | solution.py:175
  301.4 115.3 %all-gather.11.cloned.1.call-start = ((), (), s32[]{:S(2)}) async-start(), calls=%async_computation.6 | async-start | bytes 2113536 | tf_op jit(solution)/shard_map/all_gather | solution.py:15
  301.7 30.2 %copy-start.18 = (f32[4096]{0:T(1024)S(1)}, f32[4096]{0:T(1024)}, u32[]{:S(2)}) copy-start(f32[4096]{0:T(1024)} %get-tuple-element.82) | copy-start | bytes 49156
  332.6 21.3 %copy-start.23 = (bf16[768,2]{0,1:T(2,128)(2,1)S(1)}, bf16[768,2]{0,1:T(2,128)(2,1)}, u32[]{:S(2)}) copy-start(bf16[768,2]{0,1:T(2,128)(2,1)} %param.33) | copy-start | bytes 9220
  354.4 198.8 %copy-start.1 = (bf16[768,768]{1,0:T(8,128)(2,1)S(1)}, bf16[768,768]{1,0:T(8,128)(2,1)}, u32[]{:S(2)}) copy-start(bf16[768,768]{1,0:T(8,128)(2,1)} %param.26) | copy-start | bytes 3538948
  356.3 63.9 %slice-start = ((f32[524288]{0:T(1024)}), f32[4096]{0:T(1024)S(1)}, s32[]{:S(2)}) async-start(f32[524288]{0:T(1024)} %all-gather.9.cloned.1.call-done), calls=%async_computation.7 | async-start | bytes 32768 | tf_op jit(solution)/shard_map/slice | solution.py:16
  (10 other events, 64.7 us)
Sparse Core Ops, SparseCore 0:
  10.4 68.9 all-gather.6
  280.4 70.5 all-gather.8
  354.0 62.6 all-gather.10
where the time goes:
time: 566 us; the launch traced here: 560 us
  local copies, waits for them, and re-layouts  233 us (41%)
  matrix products  119 us (21%)
  waiting for transfers between devices  81.6 us (14%)
  blocking collectives  64.1 us (11%)
  starting transfers between devices  38.4 us (7%)
  between operations  13.9 us (2%)
  other arithmetic  7.24 us (1%)
    dynamic_slice x127, local copies, waits for them, and re-layouts, combined_all(): lax.scan(lambda total, share: (join(total, share), None), head, tail)  127 us
    all_gather x1, blocking collectives, local(): lax.all_gather(cluster_list, ('gallery', 'query'), axis=0, tiled=True)  64.1 us
    all_gather x2, waiting for transfers between devices, combined_all(): pieces = jax.tree.map(lambda part: lax.all_gather(part, axis), value)  58.8 us
    sub x4, matrix products, local(): weights = jax.nn.softmax(scores, axis=-1).astype(jnp.bfloat16)  40.6 us
    dot_general x4, matrix products, local(): jnp.einsum('rht,thd->rhd', weights, value_rows, preferred_element_type=jn...  34.8 us
    slice x5, local copies, waits for them, and re-layouts, local(): key_rows = image_keys[number].reshape(image_tokens, HEADS, head_size)  31 us
    slice x5, local copies, waits for them, and re-layouts, local(): value_rows = image_values[number].reshape(image_tokens, HEADS, head_size)  24.4 us
    all_to_all x1, waiting for transfers between devices, local(): lax.all_to_all(cross_state.reshape(sources, slot_total, features), ('gall...  22 us
  transfers between devices with their start and end apart: 7, of which 2 were waited for; matrix products, arithmetic and copies ran while one was open for 40% of the time, Pallas kernels for 0%

commit v1 on v0

v1 whole, which is shorter than its diff:
```python
import functools

import jax
import jax.numpy as jnp
from jax import lax
from jax.experimental import pallas as pl
from jax.experimental.pallas import tpu as pltpu
from jax.sharding import PartitionSpec as P

F32 = jnp.float32
BF16 = jnp.bfloat16
MESH = pl.DeviceIdType.MESH

HEADS = 12
HEAD = 64
D = 768
FF = 3072
TLEN = 32
Q_DEV = 32
TOPK = 16
IMG_DEV = 4
IMG_TOK = 577
CAP = 5
DEVICES = 128
MEMBERS = 4
PAIRS = Q_DEV * TOPK
SLOTS = DEVICES * CAP
CHUNKS = D // 128
BLOCK = 32
INFO = CAP * CHUNKS
TILE = 64
SORTED = SLOTS + (IMG_DEV - 1) * TILE
GROUP = 256
FF_STEP = 256

norm_epsilon = 1e-06
inverse_softness_factor = 1.0 / 0.07
VMEM_LIMIT = 56 * 1024 * 1024


def iota(shape, dimension):
    return lax.broadcasted_iota(jnp.int32, shape, dimension)


def dot(left, right, left_dim=1, right_dim=0):
    return lax.dot_general(
        left, right, (((left_dim,), (right_dim,)), ((), ())), preferred_element_type=F32
    )


def layer_norm(inputs):
    centered = inputs - jnp.mean(inputs, axis=-1, keepdims=True)
    variance = jnp.mean(centered * centered, axis=-1, keepdims=True)
    return centered * lax.rsqrt(variance + norm_epsilon)


def gelu(x):
    z = jnp.abs(x) * 0.7071067811865476
    t = 1.0 / (1.0 + 0.3275911 * z)
    poly = t * (
        0.254829592
        + t * (-0.284496736 + t * (1.421413741 + t * (-1.453152027 + t * 1.061405429)))
    )
    half_tail = 0.5 * poly * jnp.exp(-z * z)
    return x * jnp.where(x < 0, half_tail, 1.0 - half_tail)


def pair_columns(pair_ref):
    pairs = pair_ref[...]
    spread = (iota((PAIRS, Q_DEV), 0) // TOPK == iota((PAIRS, Q_DEV), 1)).astype(BF16)
    place = iota((PAIRS, TOPK), 0) % TOPK == iota((PAIRS, TOPK), 1)

    def column(values):
        rows = dot(spread, values.astype(F32).astype(BF16))
        return jnp.sum(jnp.where(place, rows, 0.0), axis=1, keepdims=True)

    return column(pairs // IMG_DEV), column(pairs % IMG_DEV)


def self_kernel(
    pair_ref, text_hbm, wq_hbm, wk_hbm, wv_hbm, wo_hbm, send_ref, meta_ref,
    text, wq, wk, wv, wo, first, wide, sems,
):
    copies = [
        pltpu.make_async_copy(source, target, sems.at[number])
        for number, (source, target) in enumerate(
            ((text_hbm, text), (wq_hbm, wq), (wk_hbm, wk), (wv_hbm, wv), (wo_hbm, wo))
        )
    ]
    for copy in copies:
        copy.start()

    owner, pick = pair_columns(pair_ref)
    lane = iota((PAIRS, DEVICES), 1)
    owner_marks = lane == owner.astype(jnp.int32)
    owner_hot = owner_marks.astype(F32).astype(BF16)
    earlier = (iota((PAIRS, PAIRS), 1) < iota((PAIRS, PAIRS), 0)).astype(BF16)
    counts = dot(earlier, owner_hot)
    rank = jnp.sum(jnp.where(owner_marks, counts, 0.0), axis=1, keepdims=True)
    meta_ref[...] = jnp.where(lane == 0, owner, jnp.where(lane == 1, rank, 0.0))
    rank_int = rank.astype(jnp.int32)
    query_lane = iota((PAIRS, 256), 1)
    query_of = iota((PAIRS, 256), 0) // TOPK
    query_hot = (query_lane == rank_int * Q_DEV + query_of) & (rank_int < CAP)
    slot_query = dot(owner_hot, query_hot.astype(F32).astype(BF16), 0, 0).astype(BF16)
    pick_hot = jnp.where(lane == rank_int, pick + 1.0, 0.0).astype(BF16)
    slot_pick = dot(owner_hot, pick_hot, 0, 0)
    wide[pl.ds(INFO, DEVICES, stride=BLOCK), :] = slot_pick
    wide[pl.ds(INFO + 1, DEVICES, stride=BLOCK), :] = jnp.zeros((DEVICES, 128), F32)

    copies[0].wait()
    for n in range(Q_DEV):
        first[n : n + 1, :] = text[n * TLEN : n * TLEN + 16, :].astype(F32)[0:1, :]
    first_rows = first[...]
    copies[1].wait()
    query = dot(first_rows.astype(BF16), wq[...]).astype(BF16).astype(F32) * HEAD**-0.5
    copies[2].wait()
    copies[3].wait()
    head_mask = iota((16, D), 1) // HEAD == iota((16, D), 0)
    per_group = GROUP // TLEN
    own = iota((per_group * 16, GROUP), 0) // 16 == iota((per_group * 16, GROUP), 1) // TLEN
    contexts = []
    for group in range(Q_DEV // per_group):
        rows = text[group * GROUP : (group + 1) * GROUP, :]
        keys = dot(rows, wk[...]).astype(BF16)
        values = dot(rows, wv[...]).astype(BF16)
        part = query[group * per_group : (group + 1) * per_group, :]
        spread = jnp.where(head_mask[None], part[:, None, :], 0.0)
        spread = spread.reshape(per_group * 16, D).astype(BF16)
        scores = jnp.where(own, dot(spread, keys, 1, 1), -1e30)
        exps = jnp.exp(scores - jnp.max(scores, axis=1, keepdims=True))
        weights = (exps / jnp.sum(exps, axis=1, keepdims=True)).astype(BF16)
        mixed = dot(weights, values).reshape(per_group, 16, D)
        contexts.append(jnp.sum(jnp.where(head_mask[None], mixed, 0.0), axis=1))
    context = jnp.concatenate(contexts, axis=0).astype(BF16)
    copies[4].wait()
    state = layer_norm(first_rows + dot(context, wo[...])).astype(BF16)
    for slot in range(CAP):
        rows = dot(slot_query[:, slot * Q_DEV : (slot + 1) * Q_DEV], state)
        for chunk in range(CHUNKS):
            wide[pl.ds(slot * CHUNKS + chunk, DEVICES, stride=BLOCK), :] = rows[
                :, chunk * 128 : (chunk + 1) * 128
            ]
    send_ref[...] = wide[...].astype(BF16)


def partner(step):
    me = lax.axis_index("gallery") * MEMBERS + lax.axis_index("query")
    other = (me + step) % DEVICES
    return me, other, (other // MEMBERS, other % MEMBERS)


def greet_all():
    barrier = pltpu.get_barrier_semaphore()

    def greet(step, carry):
        _, _, place = partner(step)
        pl.semaphore_signal(barrier, inc=1, device_id=place, device_id_type=MESH)
        return carry

    lax.fori_loop(1, DEVICES, greet, 0)
    pl.semaphore_wait(barrier, DEVICES - 1)


def exchange_kernel(send_ref, got_ref, own_sem, send_sem, got_sem):
    me, _, _ = partner(0)
    mine = pl.ds(pl.multiple_of(me * BLOCK, BLOCK), BLOCK)
    own = pltpu.make_async_copy(send_ref.at[mine, :], got_ref.at[mine, :], own_sem)
    own.start()
    greet_all()

    def push(step, carry):
        _, other, place = partner(step)
        theirs = pl.ds(pl.multiple_of(other * BLOCK, BLOCK), BLOCK)
        pltpu.make_async_remote_copy(
            src_ref=send_ref.at[theirs, :],
            dst_ref=got_ref.at[mine, :],
            send_sem=send_sem,
            recv_sem=got_sem,
            device_id=place,
            device_id_type=MESH,
        ).start()
        return carry

    lax.fori_loop(1, DEVICES, push, 0)
    own.wait()
    most = pl.ds(0, (DEVICES - 1) * BLOCK)
    pltpu.make_async_copy(send_ref.at[most, :], send_ref.at[most, :], send_sem).wait()
    pltpu.make_async_copy(got_ref.at[most, :], got_ref.at[most, :], got_sem).wait()


def cross_kernel(
    got_ref, head_ref, keys_hbm, values_hbm, wcq_hbm, wco_hbm, up_hbm, down_hbm, out_ref,
    wcq, wco, up, down, keys, values, wide, state, asked, context, hidden, total, sems,
):
    sources = [(wcq_hbm, wcq)]
    for image in range(IMG_DEV):
        sources.append((keys_hbm.at[image], keys.at[image]))
        sources.append((values_hbm.at[image], values.at[image]))
    sources += [(wco_hbm, wco), (up_hbm, up), (down_hbm, down)]
    copies = [
        pltpu.make_async_copy(source, target, sems.at[number])
        for number, (source, target) in enumerate(sources)
    ]
    for copy in copies:
        copy.start()

    wide[...] = got_ref[...].astype(F32)
    for slot in range(CAP):
        for chunk in range(CHUNKS):
            rows = wide[pl.ds(slot * CHUNKS + chunk, DEVICES, stride=BLOCK), :]
            state[
                slot * DEVICES : (slot + 1) * DEVICES, chunk * 128 : (chunk + 1) * 128
            ] = rows.astype(BF16)
    info = wide[pl.ds(INFO, DEVICES, stride=BLOCK), :]
    image = jnp.concatenate([info[:, slot : slot + 1] for slot in range(CAP)], axis=0)
    image = image.astype(jnp.int32) - 1

    lane = iota((SLOTS, 128), 1)
    image_marks = lane == image
    image_hot = image_marks.astype(F32).astype(BF16)
    earlier = (iota((SLOTS, SLOTS), 1) < iota((SLOTS, SLOTS), 0)).astype(F32).astype(BF16)
    counts = dot(earlier, image_hot)
    sizes = jnp.sum(image_marks.astype(F32), axis=0, keepdims=True)
    tiles = (sizes.astype(jnp.int32) + (TILE - 1)) // TILE
    tiles = jnp.broadcast_to(tiles.astype(F32), (8, 128)).astype(BF16)
    before = (iota((128, 128), 0) < iota((128, 128), 1)).astype(F32).astype(BF16)
    starts = dot(tiles, before)[0:1, :]
    target = jnp.sum(
        jnp.where(image_marks, counts + starts * TILE, 0.0), axis=1, keepdims=True
    )
    target = jnp.where(image >= 0, target, -1.0).astype(jnp.int32)
    order = (iota((SLOTS, SORTED), 1) == target).astype(F32).astype(BF16)
    start_at = [
        jnp.sum(jnp.where(iota((1, 128), 1) == number, starts, 0.0)).astype(jnp.int32)
        for number in range(1, IMG_DEV + 1)
    ]

    copies[0].wait()
    query = (dot(state[...], wcq[...]).astype(BF16).astype(F32) * HEAD**-0.5).astype(BF16)
    asked[...] = dot(order, query, 0, 0).astype(BF16)
    for copy in copies[1 : 1 + 2 * IMG_DEV]:
        copy.wait()

    lane_head = iota((1, 256), 1) // HEAD
    context[...] = jnp.zeros_like(context)

    def attend(tile, carry):
        number = sum((tile >= start).astype(jnp.int32) for start in start_at[:-1])
        rows = pl.ds(pl.multiple_of(tile * TILE, TILE), TILE)
        for group in range(D // 256):
            columns = slice(group * 256, (group + 1) * 256)
            part = asked[rows, columns].astype(F32)
            spread = jnp.concatenate(
                [jnp.where(lane_head == head, part, 0.0) for head in range(4)], axis=0
            ).astype(BF16)
            scores = dot(spread, keys[number, :, columns], 1, 1)
            exps = jnp.exp(scores - jnp.max(scores, axis=1, keepdims=True))
            weight = 1.0 / jnp.sum(exps, axis=1, keepdims=True)
            mixed = dot(exps.astype(BF16), values[number, :, columns]) * weight
            joined = jnp.where(lane_head == 0, mixed[:TILE, :], 0.0)
            for head in range(1, 4):
                joined = jnp.where(
                    lane_head == head, mixed[head * TILE : (head + 1) * TILE, :], joined
                )
            context[rows, columns] = joined.astype(BF16)
        return carry

    lax.fori_loop(0, start_at[-1], attend, 0)

    found = dot(order, context[...]).astype(BF16)
    for copy in copies[1 + 2 * IMG_DEV :]:
        copy.wait()
    crossed = layer_norm(state[...].astype(F32) + dot(found, wco[...]))
    state[...] = crossed.astype(BF16)
    total[...] = crossed.astype(BF16).astype(F32)
    steps = FF // FF_STEP

    def raise_step(step):
        columns = pl.ds(pl.multiple_of(step * FF_STEP, FF_STEP), FF_STEP)
        return gelu(dot(state[...], up[:, columns])).astype(BF16)

    def lower_step(step):
        rows = pl.ds(pl.multiple_of(step * FF_STEP, FF_STEP), FF_STEP)
        return dot(hidden[step % 2], down[rows, :])

    hidden[0] = raise_step(0)

    def feed(step, carry):
        total[...] += lower_step(step - 1)
        hidden[step % 2] = raise_step(step)
        return carry

    lax.fori_loop(1, steps, feed, 0)
    final = layer_norm(total[...] + lower_step(steps - 1)).astype(BF16)
    logits = dot(final, head_ref[...])
    margin = logits[:, 1:2] - logits[:, 0:1]
    back = jnp.zeros((DEVICES, 128), F32)
    back_lane = iota((DEVICES, 128), 1)
    for slot in range(CAP):
        back = jnp.where(
            back_lane == slot, margin[slot * DEVICES : (slot + 1) * DEVICES, :], back
        )
    out_ref[...] = back


def return_kernel(
    back_ref, meta_ref, caption_ref, list_ref, pair_ref, picture_ref, out_ref,
    got, own_sem, send_sem, got_sem,
):
    me, _, _ = partner(0)
    own = pltpu.make_async_copy(back_ref.at[me], got.at[me], own_sem)
    own.start()
    greet_all()

    def push(step, carry):
        _, other, place = partner(step)
        pltpu.make_async_remote_copy(
            src_ref=back_ref.at[other],
            dst_ref=got.at[me],
            send_sem=send_sem,
            recv_sem=got_sem,
            device_id=place,
            device_id_type=MESH,
        ).start()
        return carry

    lax.fori_loop(1, DEVICES, push, 0)

    scores = dot(caption_ref[...], picture_ref[...], 1, 1) * inverse_softness_factor
    images = scores.shape[1]
    image = iota((Q_DEV, images), 1)
    lists = list_ref[...]
    listed = image // 2 == lists[:, 0:1]
    for number in range(1, lists.shape[1]):
        listed = listed | (image // 2 == lists[:, number : number + 1])
    masked = jnp.where(listed, scores, -1e30)
    top = jnp.max(masked, axis=1, keepdims=True)
    sums = jnp.sum(jnp.where(listed, jnp.exp(masked - top), 0.0), axis=1, keepdims=True)
    itc_total = top + jnp.log(sums)
    pairs = pair_ref[...]
    pair_lane = iota((Q_DEV, TOPK), 1)
    offset = jnp.zeros((Q_DEV, TOPK), F32)
    for number in range(TOPK):
        chosen = jnp.sum(
            jnp.where(image == pairs[:, number : number + 1], scores, 0.0),
            axis=1,
            keepdims=True,
        )
        offset = jnp.where(pair_lane == number, chosen, offset)
    offset = offset - itc_total

    lane = iota((PAIRS, DEVICES), 1)
    meta = meta_ref[...]
    owner_hot = (lane == meta[:, 0:1].astype(jnp.int32)).astype(F32).astype(BF16)
    slot_marks = lane == meta[:, 1:2].astype(jnp.int32)
    place = iota((PAIRS, 128), 0) % TOPK == iota((PAIRS, 128), 1)

    own.wait()
    most = pl.ds(0, DEVICES - 1)
    pltpu.make_async_copy(back_ref.at[most], back_ref.at[most], send_sem).wait()
    pltpu.make_async_copy(got.at[most], got.at[most], got_sem).wait()
    rest = got[...].reshape(DEVICES, 128)
    chosen = jnp.zeros((PAIRS, 128), F32)
    for _ in range(3):
        piece = rest.astype(BF16)
        chosen = chosen + dot(owner_hot, piece)
        rest = rest - piece.astype(F32)
    margin = jnp.sum(jnp.where(slot_marks, chosen, 0.0), axis=1, keepdims=True)
    placed = jnp.where(place, margin, 0.0).reshape(Q_DEV, TOPK, 128)
    out_ref[...] = jnp.sum(placed, axis=1)[:, :TOPK] + offset


VMEM = pl.BlockSpec(memory_space=pltpu.VMEM)
ANY = pl.BlockSpec(memory_space=pl.ANY)


def local(
    text_states,
    caption_aligned_vector,
    cluster_list,
    pair_image,
    image_keys,
    image_values,
    picture_aligned_vector,
    w_self_q,
    w_self_k,
    w_self_v,
    w_self_o,
    w_cross_q,
    w_cross_o,
    w_up,
    w_down,
    itm_head,
):
    pictures = lax.all_gather(
        picture_aligned_vector, ("gallery", "query"), axis=0, tiled=True
    )
    plain = pltpu.CompilerParams(vmem_limit_bytes=VMEM_LIMIT)
    send, meta = pl.pallas_call(
        self_kernel,
        out_shape=(
            jax.ShapeDtypeStruct((DEVICES * BLOCK, 128), BF16),
            jax.ShapeDtypeStruct((PAIRS, 128), F32),
        ),
        in_specs=[VMEM] + [ANY] * 5,
        out_specs=(VMEM, VMEM),
        scratch_shapes=[
            pltpu.VMEM((Q_DEV * TLEN, D), BF16),
            pltpu.VMEM((D, D), BF16),
            pltpu.VMEM((D, D), BF16),
            pltpu.VMEM((D, D), BF16),
            pltpu.VMEM((D, D), BF16),
            pltpu.VMEM((Q_DEV, D), F32),
            pltpu.VMEM((DEVICES * BLOCK, 128), F32),
            pltpu.SemaphoreType.DMA((5,)),
        ],
        compiler_params=plain,
        name="self_stage",
    )(
        pair_image,
        text_states.reshape(Q_DEV * TLEN, D),
        w_self_q,
        w_self_k,
        w_self_v,
        w_self_o,
    )
    got = pl.pallas_call(
        exchange_kernel,
        out_shape=jax.ShapeDtypeStruct((DEVICES * BLOCK, 128), BF16),
        in_specs=[VMEM],
        out_specs=VMEM,
        scratch_shapes=[pltpu.SemaphoreType.DMA(())] * 3,
        compiler_params=pltpu.CompilerParams(
            collective_id=0, has_side_effects=True, vmem_limit_bytes=8 * 1024 * 1024
        ),
        name="exchange",
    )(send)
    back = pl.pallas_call(
        cross_kernel,
        out_shape=jax.ShapeDtypeStruct((DEVICES, 128), F32),
        in_specs=[VMEM, VMEM] + [ANY] * 6,
        out_specs=VMEM,
        scratch_shapes=[
            pltpu.VMEM((D, D), BF16),
            pltpu.VMEM((D, D), BF16),
            pltpu.VMEM((D, FF), BF16),
            pltpu.VMEM((FF, D), BF16),
            pltpu.VMEM((IMG_DEV, IMG_TOK, D), BF16),
            pltpu.VMEM((IMG_DEV, IMG_TOK, D), BF16),
            pltpu.VMEM((DEVICES * BLOCK, 128), F32),
            pltpu.VMEM((SLOTS, D), BF16),
            pltpu.VMEM((SORTED, D), BF16),
            pltpu.VMEM((SORTED, D), BF16),
            pltpu.VMEM((2, SLOTS, FF_STEP), BF16),
            pltpu.VMEM((SLOTS, D), F32),
            pltpu.SemaphoreType.DMA((4 + 2 * IMG_DEV,)),
        ],
        compiler_params=plain,
        name="cross_stage",
    )(got, itm_head, image_keys, image_values, w_cross_q, w_cross_o, w_up, w_down)
    return pl.pallas_call(
        return_kernel,
        out_shape=jax.ShapeDtypeStruct((Q_DEV, TOPK), F32),
        in_specs=[VMEM] * 6,
        out_specs=VMEM,
        scratch_shapes=[pltpu.VMEM((DEVICES, 1, 128), F32)]
        + [pltpu.SemaphoreType.DMA(())] * 3,
        compiler_params=pltpu.CompilerParams(
            collective_id=1, has_side_effects=True, vmem_limit_bytes=8 * 1024 * 1024
        ),
        name="give_back",
    )(
        back.reshape(DEVICES, 1, 128),
        meta,
        caption_aligned_vector,
        cluster_list,
        pair_image,
        pictures,
    )


def solution(mesh):
    sharded = ("gallery", "query")
    return jax.shard_map(
        local,
        mesh=mesh,
        in_specs=(
            P(sharded, None, None),
            P(sharded, None),
            P(sharded, None),
            P(sharded, None),
            P(sharded, None, None),
            P(sharded, None, None),
            P(sharded, None),
        )
        + (P(),) * 9,
        out_specs=P(sharded, None),
        check_vma=False,
    )
```

time: 566 us -> 163 us (0.29)
  local copies, waits for them, and re-layouts: 233 us -> 11.6 us
  matrix products: 119 us -> 0 us
  Pallas kernels: 0 us -> 88.5 us
  waiting for transfers between devices: 81.6 us -> 0 us
  starting transfers between devices: 38.4 us -> 0 us
  between operations: 13.9 us -> 0.1 us
  other arithmetic: 7.24 us -> 0 us
    dynamic_slice x127 -> x0, local copies, waits for them, and re-layouts: 127 us -> none  [combined_all(): lax.scan(lambda total, share: (join(total, share), None), head, tail)]
    pallas_call x0 -> x4, Pallas kernels: none -> 88.5 us  [the longest x1 36.7 us: local(): pl.pallas_call(cross_kernel, out_shape=jax.ShapeDtypeStruct((DEVICES, 128...]
    dot_general x15 -> x0, matrix products: 78.6 us -> none  [the longest x4 34.8 us: local(): jnp.einsum('rht,thd->rhd', weights, value_rows, preferred_element_type=jn...]
    slice x20 -> x0, local copies, waits for them, and re-layouts: 63.6 us -> none  [the longest x5 31 us: local(): key_rows = image_keys[number].reshape(image_tokens, HEADS, head_size)]
    all_gather x3 -> x0, waiting for transfers between devices: 58.8 us -> none  [the longest x2 58.8 us: combined_all(): pieces = jax.tree.map(lambda part: lax.all_gather(part, axis), value)]
    sub x4 -> x0, matrix products: 40.6 us -> none  [local(): weights = jax.nn.softmax(scores, axis=-1).astype(jnp.bfloat16)]
    all_to_all x4 -> x0, starting transfers between devices: 38.3 us -> none  [the longest x1 11.8 us: local(): lax.all_to_all(send_info, ('gallery', 'query'), split_axis=0, concat_axis...]
    all_to_all x4 -> x0, waiting for transfers between devices: 22 us -> none  [the longest x1 22 us: local(): lax.all_to_all(cross_state.reshape(sources, slot_total, features), ('gall...]
  transfers between devices with their start and end apart: 7 -> 0, of which waited for: 2 -> 0; matrix products, arithmetic and copies ran while one was open for 40% -> 0% of each run, Pallas kernels for 0% -> 0%
where the time goes in v1:
time: 163 us
  Pallas kernels  88.5 us (54%)
  blocking collectives  62.4 us (38%)
  local copies, waits for them, and re-layouts  11.6 us (7%)
    all_gather x1, blocking collectives, local(): lax.all_gather(picture_aligned_vector, ('gallery', 'query'), axis=0, tile...  62.4 us
    pallas_call x1, Pallas kernels, local(): pl.pallas_call(cross_kernel, out_shape=jax.ShapeDtypeStruct((DEVICES, 128...  36.7 us
    pallas_call x1, Pallas kernels, local(): pl.pallas_call(exchange_kernel, out_shape=jax.ShapeDtypeStruct((DEVICES *...  26.4 us
    pallas_call x1, Pallas kernels, local(): pl.pallas_call(return_kernel, out_shape=jax.ShapeDtypeStruct((Q_DEV, TOPK...  14.1 us
    pallas_call x1, Pallas kernels, local(): pl.pallas_call(self_kernel, out_shape=(jax.ShapeDtypeStruct((DEVICES * BL...  11.3 us
    unnamed x28, local copies, waits for them, and re-layouts  11 us

profile of v1, /device:TPU:1, one launch (start us, length us, event | category | flops | bytes accessed | tf_op | source)
XLA Modules:
  0.0 162.7 jit_solution(9270115030400361949)
XLA Ops:
  0.0 1.4 copy.24.pair_ref
  1.4 11.3 %self_stage.1 = (bf16[4096,128]{1,0:T(8,128)(2,1)}, f32[512,128]{1,0:T(8,128)}) custom-call(s32[32,16]{1,0:T(8,128)} %copy.24.pair_ref, bf16[1024,768]{1,0:T(8,128)(2,1)} %bitcast.4, bf16[768,768]{1,0:T(8,128)(2,1)} %wq_hbm.1, bf16[768,768]{1,0:T(8,128)(2,1)} %wk_hbm.1, bf16[768,768]{1,0:T(8,128)(2,1)} %wv_hbm.1, bf16[768,768]{1,0:T(8,128)(2,1)} %wo_hbm.1), custom_call_target="tpu_custom_call" | custom-call | tf_op jit(solution)/shard_map/self_stage/pallas_call | solution.py:400
  12.7 0.0 copy-start.1
  12.7 1.2 copy-done.1
  13.9 26.4 %exchange.1.got_ref = bf16[4096,128]{1,0:T(8,128)(2,1)S(1)} custom-call(bf16[4096,128]{1,0:T(8,128)(2,1)S(1)} %copy-done.1), custom_call_target="tpu_custom_call" | custom-call | tf_op jit(solution)/shard_map/exchange/pallas_call | solution.py:428
  40.3 0.0 copy-start
  40.3 1.0 copy-done
  41.3 0.0 copy-done.6
  41.3 2.3 %copy.26.keys_hbm = bf16[4,577,768]{2,1,0:T(8,128)(2,1)} copy(bf16[4,577,768]{2,0,1:T(4,128)(2,1)S(1)} %copy-done.6) | data formatting | bytes 7090176 | tf_op args[4]
  43.6 1.0 copy-done.7
  44.6 2.3 %copy.27.values_hbm = bf16[4,577,768]{2,1,0:T(8,128)(2,1)} copy(bf16[4,577,768]{2,0,1:T(4,128)(2,1)S(1)} %copy-done.7) | data formatting | bytes 7090176 | tf_op args[5]
  46.9 0.8 copy.25.head_ref
  47.7 0.0 copy-start.5
  47.7 36.7 %cross_stage.1 = f32[128,128]{1,0:T(8,128)} custom-call(bf16[4096,128]{1,0:T(8,128)(2,1)} %copy-done, bf16[768,2]{1,0:T(8,128)(2,1)} %copy.25.head_ref, bf16[4,577,768]{2,1,0:T(8,128)(2,1)} %copy.26.keys_hbm, bf16[4,577,768]{2,1,0:T(8,128)(2,1)} %copy.27.values_hbm, bf16[768,768]{1,0:T(8,128)(2,1)} %wcq_hbm.1, bf16[768,768]{1,0:T(8,128)(2,1)} %wco_hbm.1, ...), custom_call_target="tpu_custom_call" | custom-call | tf_op jit(solution)/shard_map/cross_stage/pallas_call | solution.py:439
  84.4 0.0 copy-done.10
  84.4 62.4 %all-gather = bf16[128,4,256]{2,1,0:T(4,128)(2,1)S(1)} all-gather(bf16[1,4,256]{2,1,0:T(4,128)(2,1)S(1)} %bitcast.5), channel_id=1, replica_groups=mesh['gallery'=32,'query'=4] {'gallery','query'}, dimensions={0}, use_global_device_ids=true | all-gather | bytes 264192 | tf_op jit(solution)/shard_map/all_gather | solution.py:396
  146.9 0.1 reshape.9.picture_ref
  146.9 0.0 copy-done.8
  146.9 0.1 copy.28.list_ref
  147.0 0.0 copy-done.3
  147.0 0.0 copy-start.2
  147.0 0.8 copy-done.2
  147.9 14.1 %give_back.1 = f32[32,16]{1,0:T(8,128)S(1)} custom-call(f32[128,1,128]{2,1,0:T(1,128)S(1)} %bitcast.3, f32[512,128]{1,0:T(8,128)S(1)} %copy-done.3, bf16[32,256]{1,0:T(8,128)(2,1)S(1)} %copy-done.5, s32[32,8]{1,0:T(8,128)S(1)} %copy.28.list_ref, s32[32,16]{1,0:T(8,128)S(1)} %copy-done.4, bf16[512,256]{1,0:T(8,128)(2,1)S(1)} %reshape.9.picture_ref), custom_call_target="tpu_custom_call" | custom-call | tf_op jit(solution)/shard_map/give_back/pallas_call | solution.py:462
  162.0 0.7 copy.30
  (10 shorter events, 0.0 us)
Async XLA Ops:
  1.4 39.9 %copy-start.6 = (bf16[4,577,768]{2,0,1:T(4,128)(2,1)S(1)}, bf16[4,577,768]{2,0,1:T(4,128)(2,1)}, u32[]{:S(2)}) copy-start(bf16[4,577,768]{2,0,1:T(4,128)(2,1)} %param.20) | copy-start | bytes 10635268
  12.7 1.2 copy-start.1
  40.3 1.0 copy-start
  41.3 3.3 %copy-start.7 = (bf16[4,577,768]{2,0,1:T(4,128)(2,1)S(1)}, bf16[4,577,768]{2,0,1:T(4,128)(2,1)}, u32[]{:S(2)}) copy-start(bf16[4,577,768]{2,0,1:T(4,128)(2,1)} %param.21) | copy-start | bytes 10635268
  44.6 2.3 %copy-start.9 = (bf16[768,2]{0,1:T(2,128)(2,1)S(1)}, bf16[768,2]{0,1:T(2,128)(2,1)}, u32[]{:S(2)}) copy-start(bf16[768,2]{0,1:T(2,128)(2,1)} %param.31) | copy-start | bytes 9220
  47.7 36.7 %copy-start.10 = (bf16[4,256]{1,0:T(4,128)(2,1)S(1)}, bf16[4,256]{1,0:T(4,128)(2,1)}, u32[]{:S(2)}) copy-start(bf16[4,256]{1,0:T(4,128)(2,1)} %param.22) | copy-start | bytes 6148
  47.7 99.2 %copy-start.8 = (s32[32,8]{0,1:T(8,128)S(1)}, s32[32,8]{0,1:T(8,128)}, u32[]{:S(2)}) copy-start(s32[32,8]{0,1:T(8,128)} %param.18) | copy-start | bytes 3076
  47.7 99.3 %copy-start.3 = (f32[512,128]{1,0:T(8,128)S(1)}, f32[512,128]{1,0:T(8,128)}, u32[]{:S(2)}) copy-start(f32[512,128]{1,0:T(8,128)} %get-tuple-element.8.meta_ref) | copy-start | bytes 786436
  47.7 99.3 %copy-start.4 = (s32[32,16]{1,0:T(8,128)S(1)}, s32[32,16]{1,0:T(8,128)}, u32[]{:S(2)}) copy-start(s32[32,16]{1,0:T(8,128)} %copy.24.pair_ref) | copy-start | bytes 6148
  47.7 99.3 %copy-start.5 = (bf16[32,256]{1,0:T(8,128)(2,1)S(1)}, bf16[32,256]{1,0:T(8,128)(2,1)}, u32[]{:S(2)}) copy-start(bf16[32,256]{1,0:T(8,128)(2,1)} %caption_ref.1) | copy-start | bytes 49156
  147.0 0.8 copy-start.2

commit v2 on v1

v2 whole, which is shorter than its diff:
```python
import functools

import jax
import jax.numpy as jnp
from jax import lax
from jax.experimental import pallas as pl
from jax.experimental.pallas import tpu as pltpu
from jax.sharding import PartitionSpec as P

F32 = jnp.float32
BF16 = jnp.bfloat16
MESH = pl.DeviceIdType.MESH

HEADS = 12
HEAD = 64
D = 768
FF = 3072
TLEN = 32
Q_DEV = 32
TOPK = 16
IMG_DEV = 4
IMG_TOK = 577
CAP = 5
DEVICES = 128
MEMBERS = 4
PAIRS = Q_DEV * TOPK
SLOTS = DEVICES * CAP
CHUNKS = D // 128
BLOCK = 32
E = 256
NLIST = 8
PLANE = 8
PICS = 16
INFO = CAP * CHUNKS
TILE = 64
TILES = SLOTS // TILE + IMG_DEV - 1
SORTED = TILES * TILE
GROUP = 256
FF_STEP = 256

norm_epsilon = 1e-06
inverse_softness_factor = 1.0 / 0.07
VMEM_LIMIT = 56 * 1024 * 1024


def iota(shape, dimension):
    return lax.broadcasted_iota(jnp.int32, shape, dimension)


def dot(left, right, left_dim=1, right_dim=0):
    return lax.dot_general(
        left, right, (((left_dim,), (right_dim,)), ((), ())), preferred_element_type=F32
    )


def layer_norm(inputs):
    centered = inputs - jnp.mean(inputs, axis=-1, keepdims=True)
    variance = jnp.mean(centered * centered, axis=-1, keepdims=True)
    return centered * lax.rsqrt(variance + norm_epsilon)


def gelu(x):
    z = jnp.abs(x) * 0.7071067811865476
    t = 1.0 / (1.0 + 0.3275911 * z)
    poly = t * (
        0.254829592
        + t * (-0.284496736 + t * (1.421413741 + t * (-1.453152027 + t * 1.061405429)))
    )
    half_tail = 0.5 * poly * jnp.exp(-z * z)
    return x * jnp.where(x < 0, half_tail, 1.0 - half_tail)


def hot(marks):
    return marks.astype(F32).astype(BF16)


def pair_columns(pairs):
    spread = hot(iota((PAIRS, TOPK), 0) // Q_DEV == iota((PAIRS, TOPK), 1))
    place = iota((PAIRS, Q_DEV), 0) % Q_DEV == iota((PAIRS, Q_DEV), 1)

    def column(values):
        rows = dot(spread, values.astype(F32).astype(BF16))
        return jnp.sum(jnp.where(place, rows, 0.0), axis=1, keepdims=True)

    return column(pairs // IMG_DEV), column(pairs % IMG_DEV)


def turned(values):
    size = values.shape[0]
    eye = hot(iota((size, size), 0) == iota((size, size), 1))
    return dot(values.astype(F32).astype(BF16), eye, 0, 0)


def position():
    return lax.axis_index("gallery") * MEMBERS + lax.axis_index("query")


def place_of(device):
    return (device // MEMBERS, device % MEMBERS)


def block_of(device, rows):
    return pl.ds(pl.multiple_of(device * rows, rows), rows)


def greet_all(me):
    barrier = pltpu.get_barrier_semaphore()

    def greet(step, carry):
        pl.semaphore_signal(
            barrier, inc=1, device_id=place_of((me + step) % DEVICES), device_id_type=MESH
        )
        return carry

    lax.fori_loop(1, DEVICES, greet, 0)


def push_all(first, last, other_of, source_of, target, send_sem, got_sem):
    def push(step, carry):
        other = other_of(step)
        pltpu.make_async_remote_copy(
            src_ref=source_of(other),
            dst_ref=target,
            send_sem=send_sem,
            recv_sem=got_sem,
            device_id=place_of(other),
            device_id_type=MESH,
        ).start()
        return carry

    lax.fori_loop(first, last, push, 0)


def wait_all(view, sem):
    pltpu.make_async_copy(view, view, sem).wait()


def sort_slots(info):
    image = jnp.concatenate([info[:, slot : slot + 1] for slot in range(CAP)], axis=0)
    image = image.astype(jnp.int32) - 1
    image_marks = iota((SLOTS, 128), 1) == image
    earlier = hot(iota((SLOTS, SLOTS), 1) < iota((SLOTS, SLOTS), 0))
    counts = dot(earlier, hot(image_marks))
    sizes = jnp.sum(image_marks.astype(F32), axis=0, keepdims=True).astype(jnp.int32)
    tiles = (sizes + (TILE - 1)) // TILE
    lane = iota((1, 128), 1)
    starts = [jnp.int32(0)]
    for number in range(IMG_DEV - 1):
        starts.append(starts[-1] + jnp.sum(jnp.where(lane == number, tiles, 0)))
    offset = jnp.zeros((1, 128), F32)
    for number in range(1, IMG_DEV):
        offset = jnp.where(lane == number, (starts[number] * TILE).astype(F32), offset)
    target = jnp.sum(jnp.where(image_marks, counts + offset, 0.0), axis=1, keepdims=True)
    target = jnp.where(image >= 0, target, -1.0).astype(jnp.int32)
    return hot(iota((SLOTS, SORTED), 1) == target), starts


def contrast(caption, lists, pairs, pictures):
    lanes = DEVICES * PLANE
    high = dot(caption[:, 128:], pictures, 1, 1)
    scores = dot(caption[:, :128], pictures, 1, 1) + pltpu.roll(high, lanes - IMG_DEV, 1)
    scores = scores * inverse_softness_factor
    lane = iota((Q_DEV, lanes), 1)
    real = lane % PLANE < IMG_DEV
    image = jnp.where(real, lane // PLANE * IMG_DEV + lane % PLANE, -2)
    listed = image // 2 == lists[:, 0:1]
    for number in range(1, NLIST):
        listed = listed | (image // 2 == lists[:, number : number + 1])
    masked = jnp.where(listed, scores, -1e30)
    top = jnp.max(masked, axis=1, keepdims=True)
    sums = jnp.sum(jnp.where(listed, jnp.exp(masked - top), 0.0), axis=1, keepdims=True)
    itc_total = top + jnp.log(sums)
    place = iota((Q_DEV, TOPK), 1)
    offset = jnp.zeros((Q_DEV, TOPK), F32)
    for number in range(TOPK):
        chosen = jnp.sum(
            jnp.where(image == pairs[:, number : number + 1], scores, 0.0),
            axis=1,
            keepdims=True,
        )
        offset = jnp.where(place == number, chosen, offset)
    return offset - itc_total


def kernel(
    pair_ref, list_ref, caption_ref, picture_ref, head_ref,
    text_hbm, wq_hbm, wk_hbm, wv_hbm, wo_hbm, wcq_hbm, keys_hbm, values_hbm, wco_hbm, up_hbm,
    down_hbm, out_ref,
    text, wq, wk, wv, wo, wcq, keys, values, wco, up, down,
    first, wide, send, got, state, asked, context, hidden, total,
    picture_near, picture_mine, picture_all, margins, margins_got, offsets, sems, link_sems,
):
    me = position()
    targets = (text, wq, wk, wv, wo, wcq, keys, values, wco, up, down)
    sources = (
        text_hbm, wq_hbm, wk_hbm, wv_hbm, wo_hbm, wcq_hbm, keys_hbm, values_hbm, wco_hbm,
        up_hbm, down_hbm,
    )
    copies = [
        pltpu.make_async_copy(source, target, sems.at[number])
        for number, (source, target) in enumerate(zip(sources, targets))
    ]
    for copy in copies:
        copy.start()
    greet_all(me)

    pairs = pair_ref[...]
    owner, pick = pair_columns(pairs)
    lane = iota((PAIRS, DEVICES), 1)
    owner_marks = lane == owner.astype(jnp.int32)
    owner_hot = hot(owner_marks)
    earlier = hot(iota((PAIRS, PAIRS), 1) < iota((PAIRS, PAIRS), 0))
    counts = dot(earlier, owner_hot)
    rank = jnp.sum(jnp.where(owner_marks, counts, 0.0), axis=1, keepdims=True)
    rank = rank.astype(jnp.int32)
    query_lane = iota((PAIRS, 256), 1)
    query_of = iota((PAIRS, 256), 0) % Q_DEV
    query_hot = (query_lane == rank * Q_DEV + query_of) & (rank < CAP)
    slot_query = dot(owner_hot, hot(query_hot), 0, 0).astype(BF16)
    pick_hot = jnp.where(lane == rank, pick + 1.0, 0.0).astype(BF16)
    slot_pick = dot(owner_hot, pick_hot, 0, 0)
    wide[pl.ds(INFO, DEVICES, stride=BLOCK), :] = slot_pick
    wide[pl.ds(INFO + 1, DEVICES, stride=BLOCK), :] = jnp.zeros((DEVICES, 128), F32)

    pictures = picture_ref[...].astype(F32)
    pictures = jnp.concatenate(
        [pictures[:, :128], pictures[:, 128:], jnp.zeros((PLANE, 128), F32)], axis=0
    ).astype(BF16)
    near = 2 * MEMBERS
    corner = me // near * near
    own_near = block_of(me % near, PICS)
    picture_mine[...] = pictures
    picture_near[own_near, :] = pictures
    pl.semaphore_wait(pltpu.get_barrier_semaphore(), DEVICES - 1)
    push_all(
        1, near, lambda step: corner + (me + step) % near, lambda other: picture_mine,
        picture_near.at[own_near, :], link_sems.at[0], link_sems.at[1],
    )

    copies[0].wait()
    for n in range(Q_DEV):
        first[n : n + 1, :] = text[n * TLEN : n * TLEN + 16, :].astype(F32)[0:1, :]
    first_rows = first[...]
    copies[1].wait()
    query = dot(first_rows.astype(BF16), wq[...]).astype(BF16).astype(F32) * HEAD**-0.5
    copies[2].wait()
    copies[3].wait()
    head_mask = iota((16, D), 1) // HEAD == iota((16, D), 0)
    per_group = GROUP // TLEN
    own = iota((per_group * 16, GROUP), 0) // 16 == iota((per_group * 16, GROUP), 1) // TLEN
    contexts = []
    for group in range(Q_DEV // per_group):
        rows = text[group * GROUP : (group + 1) * GROUP, :]
        key_rows = dot(rows, wk[...]).astype(BF16)
        value_rows = dot(rows, wv[...]).astype(BF16)
        part = query[group * per_group : (group + 1) * per_group, :]
        spread = jnp.where(head_mask[None], part[:, None, :], 0.0)
        spread = spread.reshape(per_group * 16, D).astype(BF16)
        scores = jnp.where(own, dot(spread, key_rows, 1, 1), -1e30)
        exps = jnp.exp(scores - jnp.max(scores, axis=1, keepdims=True))
        weights = (exps / jnp.sum(exps, axis=1, keepdims=True)).astype(BF16)
        mixed = dot(weights, value_rows).reshape(per_group, 16, D)
        contexts.append(jnp.sum(jnp.where(head_mask[None], mixed, 0.0), axis=1))
    self_context = jnp.concatenate(contexts, axis=0).astype(BF16)
    copies[4].wait()
    leading = layer_norm(first_rows + dot(self_context, wo[...])).astype(BF16)
    for slot in range(CAP):
        rows = dot(slot_query[:, slot * Q_DEV : (slot + 1) * Q_DEV], leading)
        for chunk in range(CHUNKS):
            wide[pl.ds(slot * CHUNKS + chunk, DEVICES, stride=BLOCK), :] = rows[
                :, chunk * 128 : (chunk + 1) * 128
            ]
    send[...] = wide[...].astype(BF16)

    mine = block_of(me, BLOCK)
    own_copy = pltpu.make_async_copy(send.at[mine, :], got.at[mine, :], link_sems.at[2])
    own_copy.start()
    push_all(
        1, DEVICES, lambda step: (me + step) % DEVICES,
        lambda other: send.at[block_of(other, BLOCK), :],
        got.at[mine, :], link_sems.at[3], link_sems.at[4],
    )

    seven = pl.ds(0, (near - 1) * PICS)
    wait_all(picture_near.at[seven, :], link_sems.at[0])
    wait_all(picture_near.at[seven, :], link_sems.at[1])
    column = near * PLANE
    gathered = jnp.concatenate(
        [
            picture_near[number * PICS : (number + 1) * PICS, :].astype(F32)[:PLANE]
            for number in range(near)
        ],
        axis=0,
    ).astype(BF16)
    own_column = block_of(me // near, column)
    picture_all[own_column, :] = gathered
    push_all(
        1, DEVICES // near, lambda step: (me + step * near) % DEVICES,
        lambda other: picture_all.at[own_column, :],
        picture_all.at[own_column, :], link_sems.at[5], link_sems.at[6],
    )
    others = pl.ds(0, (DEVICES // near - 1) * column)
    wait_all(picture_all.at[others, :], link_sems.at[5])
    wait_all(picture_all.at[others, :], link_sems.at[6])
    image_of = turned(pairs // IMG_DEV) * IMG_DEV + turned(pairs % IMG_DEV)
    offset = contrast(
        caption_ref[...],
        turned(list_ref[...]).astype(jnp.int32),
        image_of.astype(jnp.int32),
        picture_all[...],
    )
    offsets[...] = offset.T

    own_copy.wait()
    most = pl.ds(0, (DEVICES - 1) * BLOCK)
    wait_all(send.at[most, :], link_sems.at[3])
    wait_all(got.at[most, :], link_sems.at[4])

    wide[...] = got[...].astype(F32)
    for slot in range(CAP):
        for chunk in range(CHUNKS):
            rows = wide[pl.ds(slot * CHUNKS + chunk, DEVICES, stride=BLOCK), :]
            state[
                slot * DEVICES : (slot + 1) * DEVICES, chunk * 128 : (chunk + 1) * 128
            ] = rows.astype(BF16)
    order, starts = sort_slots(wide[pl.ds(INFO, DEVICES, stride=BLOCK), :])
    copies[5].wait()
    query = (dot(state[...], wcq[...]).astype(BF16).astype(F32) * HEAD**-0.5).astype(BF16)
    asked[...] = dot(order, query, 0, 0).astype(BF16)
    copies[6].wait()
    copies[7].wait()
    lane_head = iota((1, 256), 1) // HEAD

    def attend(tile, carry):
        number = sum((tile >= start).astype(jnp.int32) for start in starts[1:])
        rows = pl.ds(pl.multiple_of(tile * TILE, TILE), TILE)
        for group in range(D // 256):
            columns = slice(group * 256, (group + 1) * 256)
            part = asked[rows, columns].astype(F32)
            spread = jnp.concatenate(
                [jnp.where(lane_head == head, part, 0.0) for head in range(4)], axis=0
            ).astype(BF16)
            scores = dot(spread, keys[number, :, columns], 1, 1)
            exps = jnp.exp(scores - jnp.max(scores, axis=1, keepdims=True))
            weight = 1.0 / jnp.sum(exps, axis=1, keepdims=True)
            mixed = dot(exps.astype(BF16), values[number, :, columns]) * weight
            joined = jnp.where(lane_head == 0, mixed[:TILE, :], 0.0)
            for head in range(1, 4):
                joined = jnp.where(
                    lane_head == head, mixed[head * TILE : (head + 1) * TILE, :], joined
                )
            context[rows, columns] = joined.astype(BF16)
        return carry

    lax.fori_loop(0, TILES, attend, 0)
    found = dot(order, context[...]).astype(BF16)
    copies[8].wait()
    crossed = layer_norm(state[...].astype(F32) + dot(found, wco[...])).astype(BF16)
    state[...] = crossed
    total[...] = crossed.astype(F32)

    copies[9].wait()
    copies[10].wait()

    def raise_step(step):
        columns = pl.ds(pl.multiple_of(step * FF_STEP, FF_STEP), FF_STEP)
        return gelu(dot(state[...], up[:, columns])).astype(BF16)

    def lower_step(step):
        rows = pl.ds(pl.multiple_of(step * FF_STEP, FF_STEP), FF_STEP)
        return dot(hidden[step % 2], down[rows, :])

    hidden[0] = raise_step(0)

    def feed(step, carry):
        total[...] += lower_step(step - 1)
        hidden[step % 2] = raise_step(step)
        return carry

    steps = FF // FF_STEP
    lax.fori_loop(1, steps, feed, 0)
    final = layer_norm(total[...] + lower_step(steps - 1)).astype(BF16)
    logits = dot(final, head_ref[...], 1, 1)
    margin = logits[:, 1:2] - logits[:, 0:1]
    back = jnp.zeros((DEVICES, 128), F32)
    back_lane = iota((DEVICES, 128), 1)
    for slot in range(CAP):
        back = jnp.where(
            back_lane == slot, margin[slot * DEVICES : (slot + 1) * DEVICES, :], back
        )
    margins[...] = back.reshape(DEVICES, 1, 128)

    own_back = pltpu.make_async_copy(margins.at[me], margins_got.at[me], link_sems.at[2])
    own_back.start()
    push_all(
        1, DEVICES, lambda step: (me + step) % DEVICES, lambda other: margins.at[other],
        margins_got.at[me], link_sems.at[7], link_sems.at[8],
    )
    own_back.wait()
    rest_of = pl.ds(0, DEVICES - 1)
    wait_all(margins.at[rest_of], link_sems.at[7])
    wait_all(margins_got.at[rest_of], link_sems.at[8])
    rest = margins_got[...].reshape(DEVICES, 128)
    chosen = jnp.zeros((PAIRS, 128), F32)
    for _ in range(3):
        piece = rest.astype(BF16)
        chosen = chosen + dot(owner_hot, piece)
        rest = rest - piece.astype(F32)
    chosen = jnp.sum(jnp.where(lane == rank, chosen, 0.0), axis=1, keepdims=True)
    query_place = iota((PAIRS, 128), 0) % Q_DEV == iota((PAIRS, 128), 1)
    placed = jnp.where(query_place, chosen, 0.0).reshape(TOPK, Q_DEV, 128)
    out_ref[...] = jnp.sum(placed, axis=1)[:, :Q_DEV] + offsets[...]


VMEM = pl.BlockSpec(memory_space=pltpu.VMEM)
ANY = pl.BlockSpec(memory_space=pl.ANY)


def local(
    text_states,
    caption_aligned_vector,
    cluster_list,
    pair_image,
    image_keys,
    image_values,
    picture_aligned_vector,
    w_self_q,
    w_self_k,
    w_self_v,
    w_self_o,
    w_cross_q,
    w_cross_o,
    w_up,
    w_down,
    itm_head,
):
    square = pltpu.VMEM((D, D), BF16)
    gallery = pltpu.VMEM((IMG_DEV, IMG_TOK, D), BF16)
    blocks = pltpu.VMEM((DEVICES * BLOCK, 128), BF16)
    sorted_rows = pltpu.VMEM((SORTED, D), BF16)
    margin_rows = pltpu.VMEM((DEVICES, 1, 128), F32)
    out = pl.pallas_call(
        kernel,
        out_shape=jax.ShapeDtypeStruct((TOPK, Q_DEV), F32),
        in_specs=[VMEM] * 5 + [ANY] * 11,
        out_specs=VMEM,
        scratch_shapes=[
            pltpu.VMEM((Q_DEV * TLEN, D), BF16),
            square,
            square,
            square,
            square,
            square,
            gallery,
            gallery,
            square,
            pltpu.VMEM((D, FF), BF16),
            pltpu.VMEM((FF, D), BF16),
            pltpu.VMEM((Q_DEV, D), F32),
            pltpu.VMEM((DEVICES * BLOCK, 128), F32),
            blocks,
            blocks,
            pltpu.VMEM((SLOTS, D), BF16),
            sorted_rows,
            sorted_rows,
            pltpu.VMEM((2, SLOTS, FF_STEP), BF16),
            pltpu.VMEM((SLOTS, D), F32),
            pltpu.VMEM((2 * MEMBERS * PICS, 128), BF16),
            pltpu.VMEM((PICS, 128), BF16),
            pltpu.VMEM((DEVICES * PLANE, 128), BF16),
            margin_rows,
            margin_rows,
            pltpu.VMEM((TOPK, Q_DEV), F32),
            pltpu.SemaphoreType.DMA((11,)),
            pltpu.SemaphoreType.DMA((9,)),
        ],
        compiler_params=pltpu.CompilerParams(
            collective_id=0, has_side_effects=True, vmem_limit_bytes=VMEM_LIMIT
        ),
        name="rerank_all",
    )(
        pair_image.T,
        cluster_list.T,
        caption_aligned_vector,
        picture_aligned_vector,
        itm_head.T,
        text_states.reshape(Q_DEV * TLEN, D),
        w_self_q,
        w_self_k,
        w_self_v,
        w_self_o,
        w_cross_q,
        image_keys,
        image_values,
        w_cross_o,
        w_up,
        w_down,
    )
    return out.T


def solution(mesh):
    sharded = ("gallery", "query")
    return jax.shard_map(
        local,
        mesh=mesh,
        in_specs=(
            P(sharded, None, None),
            P(sharded, None),
            P(sharded, None),
            P(sharded, None),
            P(sharded, None, None),
            P(sharded, None, None),
            P(sharded, None),
        )
        + (P(),) * 9,
        out_specs=P(sharded, None),
        check_vma=False,
    )
```

time: 163 us -> 97.2 us (0.60)
  blocking collectives: 62.4 us -> 0 us
  local copies, waits for them, and re-layouts: 11.6 us -> 7.95 us
    all_gather x1 -> x0, blocking collectives: 62.4 us -> none  [local(): lax.all_gather(picture_aligned_vector, ('gallery', 'query'), axis=0, tile...]
    unnamed x28 -> x5, local copies, waits for them, and re-layouts: 11 us -> 7.95 us
    pallas_call x4 -> x1, Pallas kernels: 88.5 us -> 89 us  [local(): pl.pallas_call(kernel, out_shape=jax.ShapeDtypeStruct((TOPK, Q_DEV), F32)...]
where the time goes in v2:
time: 97.2 us; the launch traced here: 97 us
  Pallas kernels  89 us (92%)
  local copies, waits for them, and re-layouts  7.95 us (8%)
    pallas_call x1, Pallas kernels, local(): pl.pallas_call(kernel, out_shape=jax.ShapeDtypeStruct((TOPK, Q_DEV), F32)...  89 us
    unnamed x5, local copies, waits for them, and re-layouts  7.95 us

profile of v2, /device:TPU:1, one launch (start us, length us, event | category | flops | bytes accessed | tf_op | source)
XLA Modules:
  0.0 97.0 jit_solution(17219044369239695240)
XLA Ops:
  0.0 0.0 copy-start
  0.0 4.4 %copy.17.keys_hbm = bf16[4,577,768]{2,1,0:T(8,128)(2,1)} copy(bf16[4,577,768]{2,0,1:T(4,128)(2,1)} %param.20) | data formatting | bytes 7090176 | tf_op args[4]
  4.4 0.0 copy-done
  4.4 2.3 %copy.18.values_hbm = bf16[4,577,768]{2,1,0:T(8,128)(2,1)} copy(bf16[4,577,768]{2,0,1:T(4,128)(2,1)S(1)} %copy-done) | data formatting | bytes 7090176 | tf_op args[5]
  6.7 89.0 %rerank_all.1 = f32[16,32]{1,0:T(8,128)} custom-call(s32[16,32]{1,0:T(8,128)} %bitcast.7, s32[8,32]{1,0:T(8,128)} %bitcast.8, bf16[32,256]{1,0:T(8,128)(2,1)} %caption_ref.1, bf16[4,256]{1,0:T(4,128)(2,1)} %picture_ref.1, bf16[2,768]{1,0:T(2,128)(2,1)} %bitcast.9, bf16[1024,768]{1,0:T(8,128)(2,1)} %bitcast.5, bf16[768,768]{1,0:T(8,128)(2,1)} %wq_hbm.1, ...), custom_call_target="tpu_custom_call" | custom-call | tf_op jit(solution)/shard_map/rerank_all/pallas_call | solution.py:442
  95.7 1.3 %copy.20 = f32[32,16]{0,1:T(8,128)} copy(f32[32,16]{0,1:T(8,128)} %bitcast.6) | data formatting | bytes 4096
Async XLA Ops:
  0.0 4.4 %copy-start = (bf16[4,577,768]{2,0,1:T(4,128)(2,1)S(1)}, bf16[4,577,768]{2,0,1:T(4,128)(2,1)}, u32[]{:S(2)}) copy-start(bf16[4,577,768]{2,0,1:T(4,128)(2,1)} %param.21) | copy-start | bytes 10635268

commit v3 on v2

--- a/solution.py
+++ b/solution.py
@@ -36,7 +36,7 @@
 TILES = SLOTS // TILE + IMG_DEV - 1
 SORTED = TILES * TILE
 GROUP = 256
-FF_STEP = 256
+FF_STEP = 512
 
 norm_epsilon = 1e-06
 inverse_softness_factor = 1.0 / 0.07
@@ -60,14 +60,7 @@
 
 
 def gelu(x):
-    z = jnp.abs(x) * 0.7071067811865476
-    t = 1.0 / (1.0 + 0.3275911 * z)
-    poly = t * (
-        0.254829592
-        + t * (-0.284496736 + t * (1.421413741 + t * (-1.453152027 + t * 1.061405429)))
-    )
-    half_tail = 0.5 * poly * jnp.exp(-z * z)
-    return x * jnp.where(x < 0, half_tail, 1.0 - half_tail)
+    return 0.5 * x * (1.0 + lax.erf(x * 0.7071067811865476))
 
 
 def hot(marks):
@@ -187,8 +180,9 @@
     text_hbm, wq_hbm, wk_hbm, wv_hbm, wo_hbm, wcq_hbm, keys_hbm, values_hbm, wco_hbm, up_hbm,
     down_hbm, out_ref,
     text, wq, wk, wv, wo, wcq, keys, values, wco, up, down,
-    first, wide, send, got, state, asked, context, hidden, total,
-    picture_near, picture_mine, picture_all, margins, margins_got, offsets, sems, link_sems,
+    first, wide, send, got, state, asked, context, hidden,
+    picture_near, picture_mine, picture_all, margins, by_place, near_margins, by_corner,
+    margins_got, offsets, sems, link_sems,
 ):
     me = position()
     targets = (text, wq, wk, wv, wo, wcq, keys, values, wco, up, down)
@@ -331,9 +325,9 @@
     copies[7].wait()
     lane_head = iota((1, 256), 1) // HEAD
 
-    def attend(tile, carry):
+    for tile in range(TILES):
         number = sum((tile >= start).astype(jnp.int32) for start in starts[1:])
-        rows = pl.ds(pl.multiple_of(tile * TILE, TILE), TILE)
+        rows = slice(tile * TILE, (tile + 1) * TILE)
         for group in range(D // 256):
             columns = slice(group * 256, (group + 1) * 256)
             part = asked[rows, columns].astype(F32)
@@ -350,36 +344,18 @@
                     lane_head == head, mixed[head * TILE : (head + 1) * TILE, :], joined
                 )
             context[rows, columns] = joined.astype(BF16)
-        return carry
-
-    lax.fori_loop(0, TILES, attend, 0)
+
     found = dot(order, context[...]).astype(BF16)
     copies[8].wait()
     crossed = layer_norm(state[...].astype(F32) + dot(found, wco[...])).astype(BF16)
     state[...] = crossed
-    total[...] = crossed.astype(F32)
 
     copies[9].wait()
+    for step in range(FF // FF_STEP):
+        columns = slice(step * FF_STEP, (step + 1) * FF_STEP)
+        hidden[:, columns] = gelu(dot(state[...], up[:, columns])).astype(BF16)
     copies[10].wait()
-
-    def raise_step(step):
-        columns = pl.ds(pl.multiple_of(step * FF_STEP, FF_STEP), FF_STEP)
-        return gelu(dot(state[...], up[:, columns])).astype(BF16)
-
-    def lower_step(step):
-        rows = pl.ds(pl.multiple_of(step * FF_STEP, FF_STEP), FF_STEP)
-        return dot(hidden[step % 2], down[rows, :])
-
-    hidden[0] = raise_step(0)
-
-    def feed(step, carry):
-        total[...] += lower_step(step - 1)
-        hidden[step % 2] = raise_step(step)
-        return carry
-
-    steps = FF // FF_STEP
-    lax.fori_loop(1, steps, feed, 0)
-    final = layer_norm(total[...] + lower_step(steps - 1)).astype(BF16)
+    final = layer_norm(state[...].astype(F32) + dot(hidden[...], down[...])).astype(BF16)
     logits = dot(final, head_ref[...], 1, 1)
     margin = logits[:, 1:2] - logits[:, 0:1]
     back = jnp.zeros((DEVICES, 128), F32)
@@ -388,19 +364,40 @@
         back = jnp.where(
             back_lane == slot, margin[slot * DEVICES : (slot + 1) * DEVICES, :], back
         )
-    margins[...] = back.reshape(DEVICES, 1, 128)
-
-    own_back = pltpu.make_async_copy(margins.at[me], margins_got.at[me], link_sems.at[2])
-    own_back.start()
+    margins[...] = back
+
+    corners = DEVICES // near
+    my_place = me % near
+    my_corner = me // near
+    for place in range(near):
+        by_place[place * corners : (place + 1) * corners, :] = margins[
+            pl.ds(place, corners, stride=near), :
+        ]
+    own_row = block_of(my_place, corners)
+    near_margins[own_row, :] = by_place[own_row, :]
     push_all(
-        1, DEVICES, lambda step: (me + step) % DEVICES, lambda other: margins.at[other],
-        margins_got.at[me], link_sems.at[7], link_sems.at[8],
-    )
-    own_back.wait()
-    rest_of = pl.ds(0, DEVICES - 1)
-    wait_all(margins.at[rest_of], link_sems.at[7])
-    wait_all(margins_got.at[rest_of], link_sems.at[8])
-    rest = margins_got[...].reshape(DEVICES, 128)
+        1, near, lambda step: corner + (me + step) % near,
+        lambda other: by_place.at[block_of(other % near, corners), :],
+        near_margins.at[own_row, :], link_sems.at[7], link_sems.at[8],
+    )
+    seven = pl.ds(0, (near - 1) * corners)
+    wait_all(by_place.at[seven, :], link_sems.at[7])
+    wait_all(near_margins.at[seven, :], link_sems.at[8])
+    for place in range(corners):
+        by_corner[place * near : (place + 1) * near, :] = near_margins[
+            pl.ds(place, near, stride=corners), :
+        ]
+    own_row = block_of(my_corner, near)
+    margins_got[own_row, :] = by_corner[own_row, :]
+    push_all(
+        1, corners, lambda step: (me + step * near) % DEVICES,
+        lambda other: by_corner.at[block_of(other // near, near), :],
+        margins_got.at[own_row, :], link_sems.at[9], link_sems.at[10],
+    )
+    others = pl.ds(0, (corners - 1) * near)
+    wait_all(by_corner.at[others, :], link_sems.at[9])
+    wait_all(margins_got.at[others, :], link_sems.at[10])
+    rest = margins_got[...]
     chosen = jnp.zeros((PAIRS, 128), F32)
     for _ in range(3):
         piece = rest.astype(BF16)
@@ -438,7 +435,7 @@
     gallery = pltpu.VMEM((IMG_DEV, IMG_TOK, D), BF16)
     blocks = pltpu.VMEM((DEVICES * BLOCK, 128), BF16)
     sorted_rows = pltpu.VMEM((SORTED, D), BF16)
-    margin_rows = pltpu.VMEM((DEVICES, 1, 128), F32)
+    margin_rows = pltpu.VMEM((DEVICES, 128), F32)
     out = pl.pallas_call(
         kernel,
         out_shape=jax.ShapeDtypeStruct((TOPK, Q_DEV), F32),
@@ -463,16 +460,18 @@
             pltpu.VMEM((SLOTS, D), BF16),
             sorted_rows,
             sorted_rows,
-            pltpu.VMEM((2, SLOTS, FF_STEP), BF16),
-            pltpu.VMEM((SLOTS, D), F32),
+            pltpu.VMEM((SLOTS, FF), BF16),
             pltpu.VMEM((2 * MEMBERS * PICS, 128), BF16),
             pltpu.VMEM((PICS, 128), BF16),
             pltpu.VMEM((DEVICES * PLANE, 128), BF16),
             margin_rows,
             margin_rows,
+            margin_rows,
+            margin_rows,
+            margin_rows,
             pltpu.VMEM((TOPK, Q_DEV), F32),
             pltpu.SemaphoreType.DMA((11,)),
-            pltpu.SemaphoreType.DMA((9,)),
+            pltpu.SemaphoreType.DMA((11,)),
         ],
         compiler_params=pltpu.CompilerParams(
             collective_id=0, has_side_effects=True, vmem_limit_bytes=VMEM_LIMIT

time: 97.2 us -> 87 us (0.90)
  Pallas kernels: 89 us -> 78.5 us
    pallas_call x1, Pallas kernels: 89 us -> 78.5 us  [local(): pl.pallas_call(kernel, out_shape=jax.ShapeDtypeStruct((TOPK, Q_DEV), F32)...]
where the time goes in v3:
time: 87 us; the launch traced here: 86.5 us
  Pallas kernels  78.5 us (90%)
  local copies, waits for them, and re-layouts  7.95 us (9%)
    pallas_call x1, Pallas kernels, local(): pl.pallas_call(kernel, out_shape=jax.ShapeDtypeStruct((TOPK, Q_DEV), F32)...  78.5 us
    unnamed x5, local copies, waits for them, and re-layouts  7.95 us

profile of v3, /device:TPU:1, one launch (start us, length us, event | category | flops | bytes accessed | tf_op | source)
XLA Modules:
  0.0 86.5 jit_solution(8949912634242200173)
XLA Ops:
  0.0 0.0 copy-start
  0.0 4.4 %copy.17.keys_hbm = bf16[4,577,768]{2,1,0:T(8,128)(2,1)} copy(bf16[4,577,768]{2,0,1:T(4,128)(2,1)} %param.20) | data formatting | bytes 7090176 | tf_op args[4]
  4.4 0.0 copy-done
  4.4 2.3 %copy.18.values_hbm = bf16[4,577,768]{2,1,0:T(8,128)(2,1)} copy(bf16[4,577,768]{2,0,1:T(4,128)(2,1)S(1)} %copy-done) | data formatting | bytes 7090176 | tf_op args[5]
  6.7 78.5 %rerank_all.1 = f32[16,32]{1,0:T(8,128)} custom-call(s32[16,32]{1,0:T(8,128)} %bitcast.7, s32[8,32]{1,0:T(8,128)} %bitcast.8, bf16[32,256]{1,0:T(8,128)(2,1)} %caption_ref.1, bf16[4,256]{1,0:T(4,128)(2,1)} %picture_ref.1, bf16[2,768]{1,0:T(2,128)(2,1)} %bitcast.9, bf16[1024,768]{1,0:T(8,128)(2,1)} %bitcast.5, bf16[768,768]{1,0:T(8,128)(2,1)} %wq_hbm.1, ...), custom_call_target="tpu_custom_call" | custom-call | tf_op jit(solution)/shard_map/rerank_all/pallas_call | solution.py:439
  85.2 1.3 %copy.20 = f32[32,16]{0,1:T(8,128)} copy(f32[32,16]{0,1:T(8,128)} %bitcast.6) | data formatting | bytes 4096
Async XLA Ops:
  0.0 4.4 %copy-start = (bf16[4,577,768]{2,0,1:T(4,128)(2,1)S(1)}, bf16[4,577,768]{2,0,1:T(4,128)(2,1)}, u32[]{:S(2)}) copy-start(bf16[4,577,768]{2,0,1:T(4,128)(2,1)} %param.21) | copy-start | bytes 10635268

commit v4 on v3

--- a/solution.py
+++ b/solution.py
@@ -33,7 +33,8 @@
 PICS = 16
 INFO = CAP * CHUNKS
 TILE = 64
-TILES = SLOTS // TILE + IMG_DEV - 1
+TURNS = 2
+TILES = -(-(SLOTS // TILE + IMG_DEV - 1) // TURNS) * TURNS
 SORTED = TILES * TILE
 GROUP = 256
 FF_STEP = 512
@@ -126,6 +127,19 @@
 
 def wait_all(view, sem):
     pltpu.make_async_copy(view, view, sem).wait()
+
+
+def by_image(raw, target):
+    def turn(tokens):
+        target[:, tokens, :] = jnp.transpose(raw[tokens].astype(F32), (1, 0, 2)).astype(BF16)
+
+    def some(step, carry):
+        turn(pl.ds(pl.multiple_of(step * 64, 64), 64))
+        return carry
+
+    whole = IMG_TOK // 64
+    lax.fori_loop(0, whole, some, 0)
+    turn(slice(whole * 64, IMG_TOK))
 
 
 def sort_slots(info):
@@ -179,13 +193,13 @@
     pair_ref, list_ref, caption_ref, picture_ref, head_ref,
     text_hbm, wq_hbm, wk_hbm, wv_hbm, wo_hbm, wcq_hbm, keys_hbm, values_hbm, wco_hbm, up_hbm,
     down_hbm, out_ref,
-    text, wq, wk, wv, wo, wcq, keys, values, wco, up, down,
+    text, wq, wk, wv, wo, wcq, raw, wco, up, down, keys, values,
     first, wide, send, got, state, asked, context, hidden,
     picture_near, picture_mine, picture_all, margins, by_place, near_margins, by_corner,
-    margins_got, offsets, sems, link_sems,
+    margins_got, sems, link_sems,
 ):
     me = position()
-    targets = (text, wq, wk, wv, wo, wcq, keys, values, wco, up, down)
+    targets = (text, wq, wk, wv, wo, wcq, raw, raw, wco, up, down)
     sources = (
         text_hbm, wq_hbm, wk_hbm, wv_hbm, wo_hbm, wcq_hbm, keys_hbm, values_hbm, wco_hbm,
         up_hbm, down_hbm,
@@ -194,7 +208,7 @@
         pltpu.make_async_copy(source, target, sems.at[number])
         for number, (source, target) in enumerate(zip(sources, targets))
     ]
-    for copy in copies:
+    for copy in copies[:7] + copies[8:]:
         copy.start()
     greet_all(me)
 
@@ -225,11 +239,6 @@
     own_near = block_of(me % near, PICS)
     picture_mine[...] = pictures
     picture_near[own_near, :] = pictures
-    pl.semaphore_wait(pltpu.get_barrier_semaphore(), DEVICES - 1)
-    push_all(
-        1, near, lambda step: corner + (me + step) % near, lambda other: picture_mine,
-        picture_near.at[own_near, :], link_sems.at[0], link_sems.at[1],
-    )
 
     copies[0].wait()
     for n in range(Q_DEV):
@@ -266,6 +275,7 @@
             ]
     send[...] = wide[...].astype(BF16)
 
+    pl.semaphore_wait(pltpu.get_barrier_semaphore(), DEVICES - 1)
     mine = block_of(me, BLOCK)
     own_copy = pltpu.make_async_copy(send.at[mine, :], got.at[mine, :], link_sems.at[2])
     own_copy.start()
@@ -274,6 +284,17 @@
         lambda other: send.at[block_of(other, BLOCK), :],
         got.at[mine, :], link_sems.at[3], link_sems.at[4],
     )
+
+    push_all(
+        1, near, lambda step: corner + (me + step) % near, lambda other: picture_mine,
+        picture_near.at[own_near, :], link_sems.at[0], link_sems.at[1],
+    )
+
+    copies[6].wait()
+    by_image(raw, keys)
+    copies[7].start()
+    copies[7].wait()
+    by_image(raw, values)
 
     seven = pl.ds(0, (near - 1) * PICS)
     wait_all(picture_near.at[seven, :], link_sems.at[0])
@@ -293,18 +314,6 @@
         lambda other: picture_all.at[own_column, :],
         picture_all.at[own_column, :], link_sems.at[5], link_sems.at[6],
     )
-    others = pl.ds(0, (DEVICES // near - 1) * column)
-    wait_all(picture_all.at[others, :], link_sems.at[5])
-    wait_all(picture_all.at[others, :], link_sems.at[6])
-    image_of = turned(pairs // IMG_DEV) * IMG_DEV + turned(pairs % IMG_DEV)
-    offset = contrast(
-        caption_ref[...],
-        turned(list_ref[...]).astype(jnp.int32),
-        image_of.astype(jnp.int32),
-        picture_all[...],
-    )
-    offsets[...] = offset.T
-
     own_copy.wait()
     most = pl.ds(0, (DEVICES - 1) * BLOCK)
     wait_all(send.at[most, :], link_sems.at[3])
@@ -321,29 +330,32 @@
     copies[5].wait()
     query = (dot(state[...], wcq[...]).astype(BF16).astype(F32) * HEAD**-0.5).astype(BF16)
     asked[...] = dot(order, query, 0, 0).astype(BF16)
-    copies[6].wait()
-    copies[7].wait()
     lane_head = iota((1, 256), 1) // HEAD
 
-    for tile in range(TILES):
-        number = sum((tile >= start).astype(jnp.int32) for start in starts[1:])
-        rows = slice(tile * TILE, (tile + 1) * TILE)
-        for group in range(D // 256):
-            columns = slice(group * 256, (group + 1) * 256)
-            part = asked[rows, columns].astype(F32)
-            spread = jnp.concatenate(
-                [jnp.where(lane_head == head, part, 0.0) for head in range(4)], axis=0
-            ).astype(BF16)
-            scores = dot(spread, keys[number, :, columns], 1, 1)
-            exps = jnp.exp(scores - jnp.max(scores, axis=1, keepdims=True))
-            weight = 1.0 / jnp.sum(exps, axis=1, keepdims=True)
-            mixed = dot(exps.astype(BF16), values[number, :, columns]) * weight
-            joined = jnp.where(lane_head == 0, mixed[:TILE, :], 0.0)
-            for head in range(1, 4):
-                joined = jnp.where(
-                    lane_head == head, mixed[head * TILE : (head + 1) * TILE, :], joined
-                )
-            context[rows, columns] = joined.astype(BF16)
+    def attend(turn, carry):
+        for turn_tile in range(TILES // TURNS):
+            tile = turn * (TILES // TURNS) + turn_tile
+            number = sum((tile >= start).astype(jnp.int32) for start in starts[1:])
+            rows = pl.ds(pl.multiple_of(tile * TILE, TILE), TILE)
+            for group in range(D // 256):
+                columns = slice(group * 256, (group + 1) * 256)
+                part = asked[rows, columns].astype(F32)
+                spread = jnp.concatenate(
+                    [jnp.where(lane_head == head, part, 0.0) for head in range(4)], axis=0
+                ).astype(BF16)
+                scores = dot(spread, keys[number, :, columns], 1, 1)
+                exps = jnp.exp(scores - jnp.max(scores, axis=1, keepdims=True))
+                weight = 1.0 / jnp.sum(exps, axis=1, keepdims=True)
+                mixed = dot(exps.astype(BF16), values[number, :, columns]) * weight
+                joined = jnp.where(lane_head == 0, mixed[:TILE, :], 0.0)
+                for head in range(1, 4):
+                    joined = jnp.where(
+                        lane_head == head, mixed[head * TILE : (head + 1) * TILE, :], joined
+                    )
+                context[rows, columns] = joined.astype(BF16)
+        return carry
+
+    lax.fori_loop(0, TURNS, attend, 0)
 
     found = dot(order, context[...]).astype(BF16)
     copies[8].wait()
@@ -380,6 +392,17 @@
         lambda other: by_place.at[block_of(other % near, corners), :],
         near_margins.at[own_row, :], link_sems.at[7], link_sems.at[8],
     )
+    distant = pl.ds(0, (DEVICES // near - 1) * column)
+    wait_all(picture_all.at[distant, :], link_sems.at[5])
+    wait_all(picture_all.at[distant, :], link_sems.at[6])
+    image_of = turned(pairs // IMG_DEV) * IMG_DEV + turned(pairs % IMG_DEV)
+    offset = contrast(
+        caption_ref[...],
+        turned(list_ref[...]).astype(jnp.int32),
+        image_of.astype(jnp.int32),
+        picture_all[...],
+    )
+    offset = offset.T
     seven = pl.ds(0, (near - 1) * corners)
     wait_all(by_place.at[seven, :], link_sems.at[7])
     wait_all(near_margins.at[seven, :], link_sems.at[8])
@@ -406,7 +429,7 @@
     chosen = jnp.sum(jnp.where(lane == rank, chosen, 0.0), axis=1, keepdims=True)
     query_place = iota((PAIRS, 128), 0) % Q_DEV == iota((PAIRS, 128), 1)
     placed = jnp.where(query_place, chosen, 0.0).reshape(TOPK, Q_DEV, 128)
-    out_ref[...] = jnp.sum(placed, axis=1)[:, :Q_DEV] + offsets[...]
+    out_ref[...] = jnp.sum(placed, axis=1)[:, :Q_DEV] + offset
 
 
 VMEM = pl.BlockSpec(memory_space=pltpu.VMEM)
@@ -433,6 +456,7 @@
 ):
     square = pltpu.VMEM((D, D), BF16)
     gallery = pltpu.VMEM((IMG_DEV, IMG_TOK, D), BF16)
+    by_token = pltpu.VMEM((IMG_TOK, IMG_DEV, D), BF16)
     blocks = pltpu.VMEM((DEVICES * BLOCK, 128), BF16)
     sorted_rows = pltpu.VMEM((SORTED, D), BF16)
     margin_rows = pltpu.VMEM((DEVICES, 128), F32)
@@ -448,11 +472,12 @@
             square,
             square,
             square,
-            gallery,
-            gallery,
+            by_token,
             square,
             pltpu.VMEM((D, FF), BF16),
             pltpu.VMEM((FF, D), BF16),
+            gallery,
+            gallery,
             pltpu.VMEM((Q_DEV, D), F32),
             pltpu.VMEM((DEVICES * BLOCK, 128), F32),
             blocks,
@@ -469,7 +494,6 @@
             margin_rows,
             margin_rows,
             margin_rows,
-            pltpu.VMEM((TOPK, Q_DEV), F32),
             pltpu.SemaphoreType.DMA((11,)),
             pltpu.SemaphoreType.DMA((11,)),
         ],
@@ -489,8 +513,8 @@
         w_self_v,
         w_self_o,
         w_cross_q,
-        image_keys,
-        image_values,
+        jnp.transpose(image_keys, (1, 0, 2)),
+        jnp.transpose(image_values, (1, 0, 2)),
         w_cross_o,
         w_up,
         w_down,

time: 87 us -> 75.2 us (0.86)
  local copies, waits for them, and re-layouts: 7.95 us -> 1.3 us
  Pallas kernels: 78.5 us -> 73.7 us
    unnamed x5 -> x1, local copies, waits for them, and re-layouts: 7.95 us -> 1.3 us
    pallas_call x1, Pallas kernels: 78.5 us -> 73.7 us  [local(): pl.pallas_call(kernel, out_shape=jax.ShapeDtypeStruct((TOPK, Q_DEV), F32)...]
where the time goes in v4:
time: 75.2 us; the launch traced here: 75 us
  Pallas kernels  73.7 us (98%)
  local copies, waits for them, and re-layouts  1.3 us (2%)
    pallas_call x1, Pallas kernels, local(): pl.pallas_call(kernel, out_shape=jax.ShapeDtypeStruct((TOPK, Q_DEV), F32)...  73.7 us

profile of v4, /device:TPU:1, one launch (start us, length us, event | category | flops | bytes accessed | tf_op | source)
XLA Modules:
  0.0 75.0 jit_solution(16348433910003280828)
XLA Ops:
  0.0 73.7 %rerank_all.1 = f32[16,32]{1,0:T(8,128)} custom-call(s32[16,32]{1,0:T(8,128)} %bitcast.11, s32[8,32]{1,0:T(8,128)} %bitcast.12, bf16[32,256]{1,0:T(8,128)(2,1)} %caption_ref.1, bf16[4,256]{1,0:T(4,128)(2,1)} %picture_ref.1, bf16[2,768]{1,0:T(2,128)(2,1)} %bitcast.13, bf16[1024,768]{1,0:T(8,128)(2,1)} %bitcast.9, bf16[768,768]{1,0:T(8,128)(2,1)} %wq_hbm.1, ...), custom_call_target="tpu_custom_call" | custom-call | tf_op jit(solution)/shard_map/rerank_all/pallas_call | solution.py:463
  73.7 1.3 %copy.18 = f32[32,16]{0,1:T(8,128)} copy(f32[32,16]{0,1:T(8,128)} %bitcast.10) | data formatting | bytes 4096

commit v5 on v4

--- a/solution.py
+++ b/solution.py
@@ -90,7 +90,7 @@
 
 
 def place_of(device):
-    return (device // MEMBERS, device % MEMBERS)
+    return (lax.div(device, MEMBERS), lax.rem(device, MEMBERS))
 
 
 def block_of(device, rows):
@@ -102,7 +102,7 @@
 
     def greet(step, carry):
         pl.semaphore_signal(
-            barrier, inc=1, device_id=place_of((me + step) % DEVICES), device_id_type=MESH
+            barrier, inc=1, device_id=place_of(lax.rem(me + step, DEVICES)), device_id_type=MESH
         )
         return carry
 
@@ -280,13 +280,13 @@
     own_copy = pltpu.make_async_copy(send.at[mine, :], got.at[mine, :], link_sems.at[2])
     own_copy.start()
     push_all(
-        1, DEVICES, lambda step: (me + step) % DEVICES,
+        1, DEVICES, lambda step: lax.rem(me + step * 37, DEVICES),
         lambda other: send.at[block_of(other, BLOCK), :],
         got.at[mine, :], link_sems.at[3], link_sems.at[4],
     )
 
     push_all(
-        1, near, lambda step: corner + (me + step) % near, lambda other: picture_mine,
+        1, near, lambda step: corner + lax.rem(me + step, near), lambda other: picture_mine,
         picture_near.at[own_near, :], link_sems.at[0], link_sems.at[1],
     )
 
@@ -310,7 +310,7 @@
     own_column = block_of(me // near, column)
     picture_all[own_column, :] = gathered
     push_all(
-        1, DEVICES // near, lambda step: (me + step * near) % DEVICES,
+        1, DEVICES // near, lambda step: lax.rem(me + step * near, DEVICES),
         lambda other: picture_all.at[own_column, :],
         picture_all.at[own_column, :], link_sems.at[5], link_sems.at[6],
     )
@@ -388,7 +388,7 @@
     own_row = block_of(my_place, corners)
     near_margins[own_row, :] = by_place[own_row, :]
     push_all(
-        1, near, lambda step: corner + (me + step) % near,
+        1, near, lambda step: corner + lax.rem(me + step, near),
         lambda other: by_place.at[block_of(other % near, corners), :],
         near_margins.at[own_row, :], link_sems.at[7], link_sems.at[8],
     )
@@ -413,7 +413,7 @@
     own_row = block_of(my_corner, near)
     margins_got[own_row, :] = by_corner[own_row, :]
     push_all(
-        1, corners, lambda step: (me + step * near) % DEVICES,
+        1, corners, lambda step: lax.rem(me + step * near, DEVICES),
         lambda other: by_corner.at[block_of(other // near, near), :],
         margins_got.at[own_row, :], link_sems.at[9], link_sems.at[10],
     )

time: 75.2 us -> 70.5 us (0.938)
  Pallas kernels: 73.7 us -> 68.9 us
    pallas_call x1, Pallas kernels: 73.7 us -> 68.9 us  [local(): pl.pallas_call(kernel, out_shape=jax.ShapeDtypeStruct((TOPK, Q_DEV), F32)...]
where the time goes in v5:
time: 70.5 us; the launch traced here: 70.2 us
  Pallas kernels  68.9 us (98%)
  local copies, waits for them, and re-layouts  1.3 us (2%)
    pallas_call x1, Pallas kernels, local(): pl.pallas_call(kernel, out_shape=jax.ShapeDtypeStruct((TOPK, Q_DEV), F32)...  68.9 us

profile of v5, /device:TPU:1, one launch (start us, length us, event | category | flops | bytes accessed | tf_op | source)
XLA Modules:
  0.0 70.2 jit_solution(5232601921691162805)
XLA Ops:
  0.0 68.9 %rerank_all.1 = f32[16,32]{1,0:T(8,128)} custom-call(s32[16,32]{1,0:T(8,128)} %bitcast.11, s32[8,32]{1,0:T(8,128)} %bitcast.12, bf16[32,256]{1,0:T(8,128)(2,1)} %caption_ref.1, bf16[4,256]{1,0:T(4,128)(2,1)} %picture_ref.1, bf16[2,768]{1,0:T(2,128)(2,1)} %bitcast.13, bf16[1024,768]{1,0:T(8,128)(2,1)} %bitcast.9, bf16[768,768]{1,0:T(8,128)(2,1)} %wq_hbm.1, ...), custom_call_target="tpu_custom_call" | custom-call | tf_op jit(solution)/shard_map/rerank_all/pallas_call | solution.py:463
  68.9 1.3 %copy.18 = f32[32,16]{0,1:T(8,128)} copy(f32[32,16]{0,1:T(8,128)} %bitcast.10) | data formatting | bytes 4096
